TPU v7x, 32 devices: a whole 2x2x4 slice. The times are simulated.
32 devices in a mesh: leaf: 32 (over z, y, x, core).
Axes of the slice: x: 2, y: 2, z: 4, core: 2. Of those that a mesh axis runs over, the one named last changes fastest.
Arguments:
- points: bfloat16 [262144, 128], P('leaf'), may hold values from -6 to 6
- leaf_basis: bfloat16 [4096, 64, 32], P('leaf'), may hold values from -0.75 to 0.75
- local_transfer: bfloat16 [8160, 32, 32], P('leaf'), may hold values from -0.75 to 0.75
- top_transfer: bfloat16 [32, 32, 32], replicated, may hold values from -0.75 to 0.75
- local_coupling: bfloat16 [8160, 8, 32, 32], P('leaf'), may hold values from -0.375 to 0.375
- local_lists: int32 [8160, 8], P('leaf'), may hold values from -1 to 4095, as said below
- top_coupling: bfloat16 [32, 8, 32, 32], replicated, may hold values from -0.375 to 0.375
- top_lists: int32 [32, 8], replicated, may hold values from -1 to 31, as said below
- near_blocks: bfloat16 [4096, 6, 64, 64], P('leaf'), may hold values from -0.3125 to 0.3125
- near_lists: int32 [4096, 6], P('leaf'), may hold values from -1 to 4095, as said below
Outputs:
- product: bfloat16 [262144, 128], P('leaf')
Inputs may be any that keep to these rules, and one draw needn't show every extreme that they name: `local_lists`: space is cut into 32 slabs one leaf box thick, subtree d being slab d; inside a slab the tree halves the cross-section alternately along its two directions, and a node at depth TD + k is a cell of that level's grid. Partners are children of the node's parent's neighbouring cells (in slabs d - 1, d, d + 1) that are not adjacent to the node; they are distinct within a row, and rows at depths TD to TD + 2 are empty. `top_lists`: rows of nodes at depths 0 and 1 are empty; other partners are distinct nodes of the same depth, two or more positions away from the node. `near_lists`: slot 0 is the leaf itself; the others are distinct leaves whose boxes touch the leaf's box, in the leaf's own slab or the slabs beside it.
All inputs are finite; a program needn't handle non-finite values.
Results may differ from a plain program's by a relative error of at most 0.028.
Values may be sent and summed in bfloat16 or wider, within the bound.
A program may use at most 192 MiB of HBM per device.

v0:
```python
import jax
import jax.numpy as jnp
from jax import lax
from jax.sharding import PartitionSpec as P


def with_halo(shard, sides, width):
    for axis, dim in sides:
        count, length = (lax.axis_size(axis), shard.shape[dim])
        up = [(i, (i + 1) % count) for i in range(count - 1)]
        down = [(j, i) for i, j in up]
        last = lax.slice_in_dim(shard, length - width, length, axis=dim)
        first = lax.slice_in_dim(shard, 0, width, axis=dim)
        before = lax.ppermute(last, axis, up)
        after = lax.ppermute(first, axis, down)
        shard = jnp.concatenate([before, shard, after], axis=dim)
    return shard


def couple(window, blocks, partner_ids, first_node):
    is_valid = partner_ids >= 0
    positions = jnp.where(is_valid, partner_ids - first_node, 0)
    total = jnp.zeros((blocks.shape[0], blocks.shape[2], window.shape[2]), jnp.float32)
    for slot_idx in range(partner_ids.shape[1]):
        picked = window[positions[:, slot_idx]]
        picked = jnp.where(is_valid[:, slot_idx, None, None], picked, jnp.zeros((), window.dtype))
        total = total + jnp.einsum(
            "mrs,msv->mrv", blocks[:, slot_idx], picked, preferred_element_type=jnp.float32
        )
    return total


def shards(
    points,
    leaf_basis,
    local_transfer,
    top_transfer,
    local_coupling,
    local_lists,
    top_coupling,
    top_lists,
    near_blocks,
    near_lists,
):
    leaf_dev, leaf_size, rank_size = leaf_basis.shape
    vec_count = points.shape[1]
    levels_dev = leaf_dev.bit_length() - 1
    device_count = lax.axis_size("leaf")
    top_depth = device_count.bit_length() - 1
    own_index = lax.axis_index("leaf")
    leaf_rows = points.reshape(leaf_dev, leaf_size, vec_count)
    coeffs = [None] * (levels_dev + 1)
    coeffs[levels_dev] = jnp.einsum(
        "lpr,lpv->lrv", leaf_basis, leaf_rows, preferred_element_type=jnp.float32
    ).astype(jnp.bfloat16)
    for depth_now in range(levels_dev - 1, -1, -1):
        lower = 2 ** (depth_now + 1) - 1
        up_terms = jnp.einsum(
            "crs,crv->csv",
            local_transfer[lower : 2 * lower + 1],
            coeffs[depth_now + 1],
            preferred_element_type=jnp.float32,
        )
        coeffs[depth_now] = (
            up_terms.reshape(-1, 2, rank_size, vec_count).sum(axis=1).astype(jnp.bfloat16)
        )
    windows = [None] * (levels_dev + 1)
    for depth_now in range(levels_dev, 2, -1):
        windows[depth_now] = with_halo(
            coeffs[depth_now], (("leaf", 0),), coeffs[depth_now].shape[0]
        )
    root_term = jnp.einsum(
        "rs,rv->sv", local_transfer[0], coeffs[0][0], preferred_element_type=jnp.float32
    )
    gathered = lax.all_gather(root_term[None], "leaf", axis=0, tiled=True)
    top_coeffs = {}
    up_terms = gathered
    for depth_now in range(top_depth - 1, 1, -1):
        level_coeff = up_terms.reshape(-1, 2, rank_size, vec_count).sum(axis=1).astype(jnp.bfloat16)
        top_coeffs[depth_now] = level_coeff
        if depth_now > 2:
            transfers = top_transfer[2**depth_now : 2 ** (depth_now + 1)]
            up_terms = jnp.einsum(
                "crs,crv->csv", transfers, level_coeff, preferred_element_type=jnp.float32
            )
    carried = None
    for depth_now in range(2, top_depth):
        ancestor = (device_count + own_index) // 2 ** (top_depth - depth_now)
        far_now = couple(
            top_coeffs[depth_now],
            top_coupling[ancestor][None],
            top_lists[ancestor][None],
            2**depth_now,
        )[0]
        if carried is None:
            carried = far_now
        else:
            carried = far_now + jnp.dot(
                top_transfer[ancestor],
                carried.astype(jnp.bfloat16),
                preferred_element_type=jnp.float32,
            )
    near_window = with_halo(leaf_rows, (("leaf", 0),), leaf_dev)
    for depth_now in range(levels_dev + 1):
        lower = 2**depth_now - 1
        parents = jnp.repeat(
            carried.astype(jnp.bfloat16).reshape(-1, rank_size, vec_count), 2, axis=0
        )
        if depth_now == 0:
            parents = parents[:1]
        carried = jnp.einsum(
            "crs,csv->crv",
            local_transfer[lower : 2 * lower + 1],
            parents,
            preferred_element_type=jnp.float32,
        )
        if depth_now >= 3:
            first_node = (own_index - 1) * (lower + 1)
            carried = carried + couple(
                windows[depth_now],
                local_coupling[lower : 2 * lower + 1],
                local_lists[lower : 2 * lower + 1],
                first_node,
            )
    far_rows = jnp.einsum(
        "lpr,lrv->lpv", leaf_basis, carried.astype(jnp.bfloat16), preferred_element_type=jnp.float32
    )
    first_leaf = (own_index - 1) * leaf_dev
    near_rows = couple(near_window, near_blocks, near_lists, first_leaf)
    return (far_rows + near_rows).astype(jnp.bfloat16).reshape(leaf_dev * leaf_size, vec_count)


def solution(mesh):
    return jax.shard_map(
        shards,
        mesh=mesh,
        in_specs=(
            P("leaf", None),
            P("leaf", None, None),
            P("leaf", None, None),
            P(),
            P("leaf", None, None, None),
            P("leaf", None),
            P(),
            P(),
            P("leaf", None, None, None),
            P("leaf", None),
        ),
        out_specs=P("leaf", None),
        check_vma=False,
    )
```

profile of v0, /device:TPU:0, one launch (start us, length us, event | category | flops | bytes accessed | tf_op | source)
XLA Modules:
  0.0 520.1 jit_solution(6225380058709726750)
XLA Ops:
  3.4 1.9 slice.731
  8.6 2.7 copy.140
  11.3 3.7 copy.65
  15.0 3.6 convolution_convert_fusion
  25.5 3.6 collective-permute-start
  30.5 5.2 collective-permute-start.2
  74.5 3.7 fusion.554
  78.2 2.1 fusion.553
  80.3 2.0 fusion.552
  82.3 2.1 slice_bitcast_fusion
  84.4 2.0 fusion.551
  101.9 1.9 copy.136
  103.9 1.9 copy.135
  110.8 47.9 %all-gather = f32[1024,128]{1,0:T(8,128)} all-gather(f32[32,128]{1,0:T(8,128)S(1)} %fusion.46), channel_id=2, replica_groups=mesh['leaf'=32] {'leaf'}, dimensions={0}, use_global_device_ids=true | all-gather | bytes 540672 | tf_op jit(solution)/shard_map/all_gather | solution.py:75
  193.8 2.1 convolution_add_fusion.38
  203.1 2.3 fusion.48
  226.0 1.9 copy.153
  240.5 2.6 copy.132
  243.1 2.7 copy.125
  245.8 2.7 copy.126
  248.5 3.1 copy.127
  251.5 2.6 copy.128
  254.1 2.6 copy.129
  256.7 2.6 copy.130
  259.3 2.6 copy.131
  274.2 6.8 %fusion.550 = (bf16[128,1,64,64]{0,3,2,1:T(8,128)(2,1)}, bf16[128,1,64,64]{0,3,2,1:T(8,128)(2,1)}, bf16[128,1,64,64]{0,3,2,1:T(8,128)(2,1)}, bf16[128,1,64,64]{0...) fusion(bf16[128,6,64,64]{0,3,2,1:T(8,128)(2,1)} %param.18), kind=kLoop, calls=%fused_computation.806 | loop fusion | bytes 12582912 | tf_op jit(solution)/shard_map/slice | solution.py:28
  281.0 4.7 copy.180
  285.8 4.7 copy.179
  290.5 4.7 copy.178
  295.2 4.7 copy.177
  299.9 3.8 copy.176
  304.0 3.7 copy.175
  316.8 3.0 collective-permute-start.4
  328.7 3.9 collective-permute-start.6
  350.9 4.0 collective-permute-start.8
  374.5 4.5 collective-permute-start.10
  401.8 3.5 pad_maximum_fusion.1
  405.3 3.7 gather_fusion.39
  409.0 2.8 gather_fusion.38
  411.7 3.7 gather_fusion.37
  415.4 3.7 gather_fusion.36
  419.1 3.7 gather_fusion.35
  422.7 3.7 gather_fusion.34
  426.4 3.8 gather_fusion.33
  430.2 3.7 gather_fusion.32
  433.9 3.4 fusion.71
  437.3 2.0 fusion.69
  439.4 2.1 fusion.67
  441.5 2.0 fusion.65
  443.5 2.0 fusion.63
  445.5 2.0 fusion.61
  447.5 2.0 fusion.59
  449.5 10.5 %fusion.23 = f32[128,128,64]{1,2,0:T(8,128)} fusion(bf16[128,64,32]{1,2,0:T(8,128)(2,1)S(1)} %copy-done.3, f32[128,128,32]{1,2,0:T(8,128)} %fusion.565, f32[128,128,32]{1,2,0:T(8,128)} %fusion.59, f32[128,128,32]{1,2,0:T(8,128)} %fusion.61, f32[128,128,32]{1,2,0:T(8,128)} %fusion.63, f32[128,128,32]{1,2,0:T(8,128)} %fusion.65, f32[128,128,32]{1,2,0:T(8,128)} %fusion.67, ...), kind=kOutput, calls=%fused_computation.74 | convolution fusion | flops 105906176 | bytes 22806656 | tf_op jit(solution)/shard_map/lpr,lrv->lpv/dot_general | solution.py:125
  460.0 6.4 %pad_maximum_fusion = bf16[384,64,128]{2,1,0:T(8,128)(2,1)} fusion(bf16[128,64,128]{2,1,0:T(8,128)(2,1)} %collective-permute-done.11, bf16[128,64,128]{2,1,0:T(8,128)(2,1)} %bitcast.2, bf16[128,64,128]{2,1,0:T(8,128)(2,1)} %collective-permute-done.10), kind=kLoop, calls=%fused_computation.46 | loop fusion | flops 6291456 | bytes 12582912 | tf_op jit(solution)/shard_map/concatenate | solution.py:16
  466.5 4.9 gather_fusion.45
  471.4 5.0 gather_fusion.44
  476.4 5.0 gather_fusion.43
  481.4 5.0 gather_fusion.42
  486.5 5.0 gather_fusion.41
  491.5 5.3 %gather_fusion.40 = bf16[128,64,128]{2,1,0:T(8,128)(2,1)} fusion(bf16[384,64,128]{2,1,0:T(8,128)(2,1)} %pad_maximum_fusion, s32[1024]{0:T(1024)} %pad_clamp_fusion.5), kind=kCustom, calls=%fused_computation.40 | custom fusion | bytes 4194816 | tf_op jit(solution)/shard_map/gather | solution.py:25
  496.8 2.5 fusion.1
  504.1 2.8 fusion.7
  507.5 2.7 fusion.9
  510.3 9.4 %add_convert_fusion = bf16[128,128,64]{1,2,0:T(8,128)(2,1)} fusion(f32[128,128,64]{1,2,0:T(8,128)} %fusion.23, f32[128,128,64]{1,2,0:T(8,128)S(1)} %fusion.1, f32[128,128,64]{1,2,0:T(8,128)S(1)} %fusion.3, f32[128,128,64]{1,2,0:T(8,128)S(1)} %fusion.5, f32[128,128,64]{1,2,0:T(8,128)} %fusion.9, f32[128,128,64]{1,2,0:T(8,128)} %fusion.7, ...), kind=kOutput, calls=%fused_computation.47 | convolution fusion | flops 142606336 | bytes 30408832 | tf_op jit(solution)/shard_map/mrs,msv->mrv/dot_general | solution.py:27
  (587 shorter events, 199.9 us)
Async XLA Ops:
  0.0 178.7 %copy-start = (bf16[32,8,32,32]{3,2,1,0:T(8,128)(2,1)S(1)}, bf16[32,8,32,32]{3,2,1,0:T(8,128)(2,1)}, u32[]{:S(2)}) copy-start(bf16[32,8,32,32]{3,2,1,0:T(8,128)(2,1)} %param.16) | copy-start | bytes 1572868
  5.9 16.4 %copy-start.30 = (bf16[32,32,32]{1,2,0:T(8,128)(2,1)}, bf16[32,32,32]{1,2,0:T(8,128)(2,1)S(1)}, u32[]{:S(2)}) copy-start(bf16[32,32,32]{1,2,0:T(8,128)(2,1)S(1)} %copy.138) | copy-start | bytes 196612
  18.6 18.5 %copy-start.110 = (s32[32,8]{0,1:T(8,128)S(1)}, s32[32,8]{0,1:T(8,128)}, u32[]{:S(2)}) copy-start(s32[32,8]{0,1:T(8,128)} %param.17) | copy-start | bytes 3076
  24.3 292.5 %collective-permute-start.1 = (bf16[8,32,128]{2,1,0:T(8,128)(2,1)}, bf16[8,32,128]{2,1,0:T(8,128)(2,1)}, u32[]{:S(2)}, u32[]{:S(2)}) collective-permute-start(bf16[8,32,128]{2,1,0:T(8,128)(2,1)} %bitcast_reduce_fusion.4), channel_id=1, source_target_pairs={{1,0},{2,1},{3,2},{4,3},{5,4},{6,5},{7,6},{8,7},{9,8},{10,9},{11,1... | collective-permute-start | bytes 196616 | tf_op jit(solution)/shard_map/ppermute | solution.py:15
  25.5 294.2 %collective-permute-start = (bf16[8,32,128]{2,1,0:T(8,128)(2,1)}, bf16[8,32,128]{2,1,0:T(8,128)(2,1)}, u32[]{:S(2)}, u32[]{:S(2)}) collective-permute-start(bf16[8,32,128]{2,1,0:T(8,128)(2,1)} %bitcast_reduce_fusion.4), channel_id=1, source_target_pairs={{0,1},{1,2},{2,3},{3,4},{4,5},{5,6},{6,7},{7,8},{8,9},{9,10},{10,1... | collective-permute-start | bytes 196616 | tf_op jit(solution)/shard_map/ppermute | solution.py:14
  29.2 299.5 %collective-permute-start.3 = (bf16[16,32,128]{2,1,0:T(8,128)(2,1)S(1)}, bf16[16,32,128]{2,1,0:T(8,128)(2,1)}, u32[]{:S(2)}, u32[]{:S(2)}) collective-permute-start(bf16[16,32,128]{2,1,0:T(8,128)(2,1)S(1)} %bitcast_reduce_fusion.2), channel_id=1, source_target_pairs={{1,0},{2,1},{3,2},{4,3},{5,4},{6,5},{7,6},{8,7},{9,8},{10,9},{11,1... | collective-permute-start | bytes 393224 | tf_op jit(solution)/shard_map/ppermute | solution.py:15
  30.5 302.1 %collective-permute-start.2 = (bf16[16,32,128]{2,1,0:T(8,128)(2,1)S(1)}, bf16[16,32,128]{2,1,0:T(8,128)(2,1)}, u32[]{:S(2)}, u32[]{:S(2)}) collective-permute-start(bf16[16,32,128]{2,1,0:T(8,128)(2,1)S(1)} %bitcast_reduce_fusion.2), channel_id=1, source_target_pairs={{0,1},{1,2},{2,3},{3,4},{4,5},{5,6},{6,7},{7,8},{8,9},{9,10},{10,1... | collective-permute-start | bytes 393224 | tf_op jit(solution)/shard_map/ppermute | solution.py:14
  35.7 315.3 %collective-permute-start.5 = (bf16[32,32,128]{2,1,0:T(8,128)(2,1)}, bf16[32,32,128]{2,1,0:T(8,128)(2,1)}, u32[]{:S(2)}, u32[]{:S(2)}) collective-permute-start(bf16[32,32,128]{2,1,0:T(8,128)(2,1)} %bitcast_reduce_fusion.1), channel_id=1, source_target_pairs={{1,0},{2,1},{3,2},{4,3},{5,4},{6,5},{7,6},{8,7},{9,8},{10,9},{11,1... | collective-permute-start | bytes 786440 | tf_op jit(solution)/shard_map/ppermute | solution.py:15
  84.4 21.4 %slice-start = ((bf16[255,32,32]{0,2,1:T(8,128)(2,1)}), bf16[1,32,32]{0,2,1:T(8,128)(2,1)S(1)}, s32[]{:S(2)}) async-start(bf16[255,32,32]{0,2,1:T(8,128)(2,1)} %param.12), calls=%async_computation | async-start | bytes 524288 | tf_op jit(solution)/shard_map/slice | solution.py:113
  159.8 19.6 %copy-start.88 = (bf16[16,32,128]{2,1,0:T(8,128)(2,1)}, bf16[16,32,128]{2,1,0:T(8,128)(2,1)S(1)}, u32[]{:S(2)}) copy-start(bf16[16,32,128]{2,1,0:T(8,128)(2,1)S(1)} %reduce_sum.91) | copy-start | bytes 393220
  162.0 39.7 %copy-start.100 = (bf16[4,32,128]{2,1,0:T(8,128)(2,1)}, bf16[4,32,128]{2,1,0:T(8,128)(2,1)S(1)}, u32[]{:S(2)}) copy-start(bf16[4,32,128]{2,1,0:T(8,128)(2,1)S(1)} %bitcast_reduce_fusion.5) | copy-start | bytes 98308
  179.4 39.3 %copy-start.65 = (bf16[8,1,32,32]{0,3,2,1:T(8,128)(2,1)S(1)}, bf16[8,1,32,32]{0,3,2,1:T(8,128)(2,1)}, u32[]{:S(2)}) copy-start(bf16[8,1,32,32]{0,3,2,1:T(8,128)(2,1)} %get-tuple-element.330) | copy-start | bytes 49156
  205.4 10.9 %copy-start.68 = (bf16[8,1,32,32]{0,3,2,1:T(8,128)(2,1)S(1)}, bf16[8,1,32,32]{0,3,2,1:T(8,128)(2,1)}, u32[]{:S(2)}) copy-start(bf16[8,1,32,32]{0,3,2,1:T(8,128)(2,1)} %get-tuple-element.327) | copy-start | bytes 49156
  205.4 11.7 %copy-start.67 = (bf16[8,1,32,32]{0,3,2,1:T(8,128)(2,1)S(1)}, bf16[8,1,32,32]{0,3,2,1:T(8,128)(2,1)}, u32[]{:S(2)}) copy-start(bf16[8,1,32,32]{0,3,2,1:T(8,128)(2,1)} %get-tuple-element.328) | copy-start | bytes 49156
  205.4 12.5 %copy-start.66 = (bf16[8,1,32,32]{0,3,2,1:T(8,128)(2,1)S(1)}, bf16[8,1,32,32]{0,3,2,1:T(8,128)(2,1)}, u32[]{:S(2)}) copy-start(bf16[8,1,32,32]{0,3,2,1:T(8,128)(2,1)} %get-tuple-element.329) | copy-start | bytes 49156
  205.4 14.1 %copy-start.79 = (bf16[16,1,32,32]{0,3,2,1:T(8,128)(2,1)S(1)}, bf16[16,1,32,32]{0,3,2,1:T(8,128)(2,1)}, u32[]{:S(2)}) copy-start(bf16[16,1,32,32]{0,3,2,1:T(8,128)(2,1)} %get-tuple-element.315) | copy-start | bytes 98308
  207.6 16.6 %copy-start.78 = (bf16[16,1,32,32]{0,3,2,1:T(8,128)(2,1)S(1)}, bf16[16,1,32,32]{0,3,2,1:T(8,128)(2,1)}, u32[]{:S(2)}) copy-start(bf16[16,1,32,32]{0,3,2,1:T(8,128)(2,1)} %get-tuple-element.318) | copy-start | bytes 98308
  209.4 15.7 %copy-start.77 = (bf16[16,1,32,32]{0,3,2,1:T(8,128)(2,1)S(1)}, bf16[16,1,32,32]{0,3,2,1:T(8,128)(2,1)}, u32[]{:S(2)}) copy-start(bf16[16,1,32,32]{0,3,2,1:T(8,128)(2,1)} %get-tuple-element.319) | copy-start | bytes 98308
  217.1 14.4 %copy-start.76 = (bf16[32,1,32,32]{0,3,2,1:T(8,128)(2,1)S(1)}, bf16[32,1,32,32]{0,3,2,1:T(8,128)(2,1)}, u32[]{:S(2)}) copy-start(bf16[32,1,32,32]{0,3,2,1:T(8,128)(2,1)} %get-tuple-element.307) | copy-start | bytes 196612
  217.9 14.8 %copy-start.75 = (bf16[32,1,32,32]{0,3,2,1:T(8,128)(2,1)S(1)}, bf16[32,1,32,32]{0,3,2,1:T(8,128)(2,1)}, u32[]{:S(2)}) copy-start(bf16[32,1,32,32]{0,3,2,1:T(8,128)(2,1)} %get-tuple-element.308) | copy-start | bytes 196612
  219.5 14.3 %copy-start.74 = (bf16[32,1,32,32]{0,3,2,1:T(8,128)(2,1)S(1)}, bf16[32,1,32,32]{0,3,2,1:T(8,128)(2,1)}, u32[]{:S(2)}) copy-start(bf16[32,1,32,32]{0,3,2,1:T(8,128)(2,1)} %get-tuple-element.309) | copy-start | bytes 196612
  220.4 14.5 %copy-start.73 = (bf16[32,1,32,32]{0,3,2,1:T(8,128)(2,1)S(1)}, bf16[32,1,32,32]{0,3,2,1:T(8,128)(2,1)}, u32[]{:S(2)}) copy-start(bf16[32,1,32,32]{0,3,2,1:T(8,128)(2,1)} %get-tuple-element.310) | copy-start | bytes 196612
  224.2 11.9 %copy-start.72 = (bf16[32,1,32,32]{0,3,2,1:T(8,128)(2,1)S(1)}, bf16[32,1,32,32]{0,3,2,1:T(8,128)(2,1)}, u32[]{:S(2)}) copy-start(bf16[32,1,32,32]{0,3,2,1:T(8,128)(2,1)} %get-tuple-element.311) | copy-start | bytes 196612
  225.1 12.1 %copy-start.71 = (bf16[32,1,32,32]{0,3,2,1:T(8,128)(2,1)S(1)}, bf16[32,1,32,32]{0,3,2,1:T(8,128)(2,1)}, u32[]{:S(2)}) copy-start(bf16[32,1,32,32]{0,3,2,1:T(8,128)(2,1)} %get-tuple-element.312) | copy-start | bytes 196612
  226.0 12.4 %copy-start.70 = (bf16[32,1,32,32]{0,3,2,1:T(8,128)(2,1)S(1)}, bf16[32,1,32,32]{0,3,2,1:T(8,128)(2,1)}, u32[]{:S(2)}) copy-start(bf16[32,1,32,32]{0,3,2,1:T(8,128)(2,1)} %get-tuple-element.313) | copy-start | bytes 196612
  303.8 9.9 %copy-start.159 = (s32[64]{0:T(128)S(1)}, s32[64]{0:T(128)}, u32[]{:S(2)}) copy-start(s32[64]{0:T(128)} %get-tuple-element.348) | copy-start | bytes 772
  303.8 10.5 %copy-start.157 = (s32[64]{0:T(128)S(1)}, s32[64]{0:T(128)}, u32[]{:S(2)}) copy-start(s32[64]{0:T(128)} %get-tuple-element.350) | copy-start | bytes 772
  303.8 10.5 %copy-start.158 = (s32[64]{0:T(128)S(1)}, s32[64]{0:T(128)}, u32[]{:S(2)}) copy-start(s32[64]{0:T(128)} %get-tuple-element.351) | copy-start | bytes 772
  303.8 11.1 %copy-start.155 = (s32[32]{0:T(128)S(1)}, s32[32]{0:T(128)}, u32[]{:S(2)}) copy-start(s32[32]{0:T(128)} %get-tuple-element.355) | copy-start | bytes 388
  303.8 11.1 %copy-start.156 = (s32[32]{0:T(128)S(1)}, s32[32]{0:T(128)}, u32[]{:S(2)}) copy-start(s32[32]{0:T(128)} %get-tuple-element.356) | copy-start | bytes 388
  303.9 11.7 %copy-start.153 = (s32[32]{0:T(128)S(1)}, s32[32]{0:T(128)}, u32[]{:S(2)}) copy-start(s32[32]{0:T(128)} %get-tuple-element.357) | copy-start | bytes 388
  303.9 11.7 %copy-start.154 = (s32[32]{0:T(128)S(1)}, s32[32]{0:T(128)}, u32[]{:S(2)}) copy-start(s32[32]{0:T(128)} %get-tuple-element.358) | copy-start | bytes 388
  303.9 12.3 %copy-start.151 = (s32[32]{0:T(128)S(1)}, s32[32]{0:T(128)}, u32[]{:S(2)}) copy-start(s32[32]{0:T(128)} %get-tuple-element.359) | copy-start | bytes 388
  303.9 12.3 %copy-start.152 = (s32[32]{0:T(128)S(1)}, s32[32]{0:T(128)}, u32[]{:S(2)}) copy-start(s32[32]{0:T(128)} %get-tuple-element.360) | copy-start | bytes 388
  303.9 12.9 %copy-start.150 = (s32[128]{0:T(128)S(1)}, s32[128]{0:T(128)}, u32[]{:S(2)}) copy-start(s32[128]{0:T(128)} %get-tuple-element.480) | copy-start | bytes 1540
  303.9 15.9 %copy-start.14 = (bf16[64,32,128]{2,1,0:T(8,128)(2,1)S(1)}, bf16[64,32,128]{2,1,0:T(8,128)(2,1)}, u32[]{:S(2)}) copy-start(bf16[64,32,128]{2,1,0:T(8,128)(2,1)} %copy-done.13) | copy-start | bytes 1572868
  303.9 22.6 %copy-start.108 = (bf16[8,1,32,32]{3,2,0,1:T(8,128)(2,1)S(1)}, bf16[8,1,32,32]{3,2,0,1:T(8,128)(2,1)}, u32[]{:S(2)}) copy-start(bf16[8,1,32,32]{3,2,0,1:T(8,128)(2,1)} %copy.144) | copy-start | bytes 49156
  303.9 22.6 %copy-start.149 = (pred[8]{0:T(512)(128)(4,1)S(1)}, pred[8]{0:T(512)(128)(4,1)}, u32[]{:S(2)}) copy-start(pred[8]{0:T(512)(128)(4,1)} %get-tuple-element.449) | copy-start | bytes 28
  303.9 22.8 %copy-start.107 = (bf16[8,1,32,32]{3,2,0,1:T(8,128)(2,1)S(1)}, bf16[8,1,32,32]{3,2,0,1:T(8,128)(2,1)}, u32[]{:S(2)}) copy-start(bf16[8,1,32,32]{3,2,0,1:T(8,128)(2,1)} %copy.143) | copy-start | bytes 49156
  303.9 22.8 %copy-start.148 = (pred[8]{0:T(512)(128)(4,1)S(1)}, pred[8]{0:T(512)(128)(4,1)}, u32[]{:S(2)}) copy-start(pred[8]{0:T(512)(128)(4,1)} %get-tuple-element.450) | copy-start | bytes 28
  303.9 23.0 %copy-start.106 = (bf16[8,1,32,32]{3,2,0,1:T(8,128)(2,1)S(1)}, bf16[8,1,32,32]{3,2,0,1:T(8,128)(2,1)}, u32[]{:S(2)}) copy-start(bf16[8,1,32,32]{3,2,0,1:T(8,128)(2,1)} %copy.145) | copy-start | bytes 49156
  304.0 23.0 %copy-start.147 = (pred[8]{0:T(512)(128)(4,1)S(1)}, pred[8]{0:T(512)(128)(4,1)}, u32[]{:S(2)}) copy-start(pred[8]{0:T(512)(128)(4,1)} %get-tuple-element.448) | copy-start | bytes 28
  307.7 19.5 %copy-start.105 = (bf16[8,1,32,32]{3,2,0,1:T(8,128)(2,1)S(1)}, bf16[8,1,32,32]{3,2,0,1:T(8,128)(2,1)}, u32[]{:S(2)}) copy-start(bf16[8,1,32,32]{3,2,0,1:T(8,128)(2,1)} %copy.146) | copy-start | bytes 49156
  307.7 19.5 %copy-start.146 = (pred[8]{0:T(512)(128)(4,1)S(1)}, pred[8]{0:T(512)(128)(4,1)}, u32[]{:S(2)}) copy-start(pred[8]{0:T(512)(128)(4,1)} %get-tuple-element.447) | copy-start | bytes 28
  307.7 19.7 %copy-start.104 = (bf16[8,1,32,32]{3,2,0,1:T(8,128)(2,1)S(1)}, bf16[8,1,32,32]{3,2,0,1:T(8,128)(2,1)}, u32[]{:S(2)}) copy-start(bf16[8,1,32,32]{3,2,0,1:T(8,128)(2,1)} %copy.147) | copy-start | bytes 49156
  307.7 19.7 %copy-start.145 = (pred[8]{0:T(512)(128)(4,1)S(1)}, pred[8]{0:T(512)(128)(4,1)}, u32[]{:S(2)}) copy-start(pred[8]{0:T(512)(128)(4,1)} %get-tuple-element.446) | copy-start | bytes 28
  307.7 20.0 %copy-start.103 = (bf16[8,1,32,32]{3,2,0,1:T(8,128)(2,1)S(1)}, bf16[8,1,32,32]{3,2,0,1:T(8,128)(2,1)}, u32[]{:S(2)}) copy-start(bf16[8,1,32,32]{3,2,0,1:T(8,128)(2,1)} %copy.148) | copy-start | bytes 49156
  307.7 20.0 %copy-start.144 = (pred[8]{0:T(512)(128)(4,1)S(1)}, pred[8]{0:T(512)(128)(4,1)}, u32[]{:S(2)}) copy-start(pred[8]{0:T(512)(128)(4,1)} %get-tuple-element.445) | copy-start | bytes 28
  307.7 20.2 %copy-start.102 = (bf16[8,1,32,32]{3,2,0,1:T(8,128)(2,1)S(1)}, bf16[8,1,32,32]{3,2,0,1:T(8,128)(2,1)}, u32[]{:S(2)}) copy-start(bf16[8,1,32,32]{3,2,0,1:T(8,128)(2,1)} %copy.149) | copy-start | bytes 49156
  307.7 20.2 %copy-start.143 = (pred[8]{0:T(512)(128)(4,1)S(1)}, pred[8]{0:T(512)(128)(4,1)}, u32[]{:S(2)}) copy-start(pred[8]{0:T(512)(128)(4,1)} %get-tuple-element.444) | copy-start | bytes 28
  313.1 15.1 %copy-start.96 = (f32[8,128,32]{1,2,0:T(8,128)S(1)}, f32[8,128,32]{1,2,0:T(8,128)}, u32[]{:S(2)}) copy-start(f32[8,128,32]{1,2,0:T(8,128)} %fusion.561) | copy-start | bytes 393220
  313.1 15.1 %copy-start.101 = (bf16[8,1,32,32]{3,2,0,1:T(8,128)(2,1)S(1)}, bf16[8,1,32,32]{3,2,0,1:T(8,128)(2,1)}, u32[]{:S(2)}) copy-start(bf16[8,1,32,32]{3,2,0,1:T(8,128)(2,1)} %copy.150) | copy-start | bytes 49156
  313.1 15.1 %copy-start.176 = (pred[8]{0:T(512)(128)(4,1)S(1)}, pred[8]{0:T(512)(128)(4,1)}, u32[]{:S(2)}) copy-start(pred[8]{0:T(512)(128)(4,1)} %get-tuple-element.443) | copy-start | bytes 28
  316.8 38.2 %collective-permute-start.4 = (bf16[32,32,128]{2,1,0:T(8,128)(2,1)}, bf16[32,32,128]{2,1,0:T(8,128)(2,1)}, u32[]{:S(2)}, u32[]{:S(2)}) collective-permute-start(bf16[32,32,128]{2,1,0:T(8,128)(2,1)} %bitcast_reduce_fusion.1), channel_id=1, source_target_pairs={{0,1},{1,2},{2,3},{3,4},{4,5},{5,6},{6,7},{7,8},{8,9},{9,10},{10,1... | collective-permute-start | bytes 786440 | tf_op jit(solution)/shard_map/ppermute | solution.py:14
  319.8 54.7 %collective-permute-start.7 = (bf16[64,32,128]{2,1,0:T(8,128)(2,1)S(1)}, bf16[64,32,128]{2,1,0:T(8,128)(2,1)}, u32[]{:S(2)}, u32[]{:S(2)}) collective-permute-start(bf16[64,32,128]{2,1,0:T(8,128)(2,1)S(1)} %copy-done.14), channel_id=1, source_target_pairs={{1,0},{2,1},{3,2},{4,3},{5,4},{6,5},{7,6},{8,7},{9,8},{10,9},{11,1... | collective-permute-start | bytes 1572872 | tf_op jit(solution)/shard_map/ppermute | solution.py:15
  328.1 15.7 %copy-start.90 = (bf16[16,1,32,32]{3,2,0,1:T(8,128)(2,1)S(1)}, bf16[16,1,32,32]{3,2,0,1:T(8,128)(2,1)}, u32[]{:S(2)}) copy-start(bf16[16,1,32,32]{3,2,0,1:T(8,128)(2,1)} %copy.152) | copy-start | bytes 98308
  328.1 15.7 %copy-start.142 = (pred[16]{0:T(512)(128)(4,1)S(1)}, pred[16]{0:T(512)(128)(4,1)}, u32[]{:S(2)}) copy-start(pred[16]{0:T(512)(128)(4,1)} %get-tuple-element.441) | copy-start | bytes 52
  328.4 15.7 %copy-start.95 = (bf16[16,1,32,32]{3,2,0,1:T(8,128)(2,1)S(1)}, bf16[16,1,32,32]{3,2,0,1:T(8,128)(2,1)}, u32[]{:S(2)}) copy-start(bf16[16,1,32,32]{3,2,0,1:T(8,128)(2,1)} %copy.151) | copy-start | bytes 98308
  328.7 50.2 %collective-permute-start.6 = (bf16[64,32,128]{2,1,0:T(8,128)(2,1)S(1)}, bf16[64,32,128]{2,1,0:T(8,128)(2,1)}, u32[]{:S(2)}, u32[]{:S(2)}) collective-permute-start(bf16[64,32,128]{2,1,0:T(8,128)(2,1)S(1)} %copy-done.14), channel_id=1, source_target_pairs={{0,1},{1,2},{2,3},{3,4},{4,5},{5,6},{6,7},{7,8},{8,9},{9,10},{10,1... | collective-permute-start | bytes 1572872 | tf_op jit(solution)/shard_map/ppermute | solution.py:14
  332.6 69.2 %collective-permute-start.9 = (bf16[128,32,128]{2,1,0:T(8,128)(2,1)}, bf16[128,32,128]{2,1,0:T(8,128)(2,1)}, u32[]{:S(2)}, u32[]{:S(2)}) collective-permute-start(bf16[128,32,128]{2,1,0:T(8,128)(2,1)} %convolution_convert_fusion), channel_id=1, source_target_pairs={{1,0},{2,1},{3,2},{4,3},{5,4},{6,5},{7,6},{8,7},{9,8},{10,9},{11,1... | collective-permute-start | bytes 3145736 | tf_op jit(solution)/shard_map/ppermute | solution.py:15
  335.1 11.2 %copy-start.94 = (bf16[16,1,32,32]{3,2,0,1:T(8,128)(2,1)S(1)}, bf16[16,1,32,32]{3,2,0,1:T(8,128)(2,1)}, u32[]{:S(2)}) copy-start(bf16[16,1,32,32]{3,2,0,1:T(8,128)(2,1)} %copy.154) | copy-start | bytes 98308
  350.9 50.8 %collective-permute-start.8 = (bf16[128,32,128]{2,1,0:T(8,128)(2,1)}, bf16[128,32,128]{2,1,0:T(8,128)(2,1)}, u32[]{:S(2)}, u32[]{:S(2)}) collective-permute-start(bf16[128,32,128]{2,1,0:T(8,128)(2,1)} %convolution_convert_fusion), channel_id=1, source_target_pairs={{0,1},{1,2},{2,3},{3,4},{4,5},{5,6},{6,7},{7,8},{8,9},{9,10},{10,1... | collective-permute-start | bytes 3145736 | tf_op jit(solution)/shard_map/ppermute | solution.py:14
  354.9 105.1 %collective-permute-start.11 = (bf16[128,64,128]{2,1,0:T(8,128)(2,1)}, bf16[128,64,128]{2,1,0:T(8,128)(2,1)}, u32[]{:S(2)}, u32[]{:S(2)}) collective-permute-start(bf16[128,64,128]{2,1,0:T(8,128)(2,1)} %bitcast.2), channel_id=1, source_target_pairs={{1,0},{2,1},{3,2},{4,3},{5,4},{6,5},{7,6},{8,7},{9,8},{10,9},{11,1... | collective-permute-start | bytes 6291464 | tf_op jit(solution)/shard_map/ppermute | solution.py:15
  374.5 85.6 %collective-permute-start.10 = (bf16[128,64,128]{2,1,0:T(8,128)(2,1)}, bf16[128,64,128]{2,1,0:T(8,128)(2,1)}, u32[]{:S(2)}, u32[]{:S(2)}) collective-permute-start(bf16[128,64,128]{2,1,0:T(8,128)(2,1)} %bitcast.2), channel_id=1, source_target_pairs={{0,1},{1,2},{2,3},{3,4},{4,5},{5,6},{6,7},{7,8},{8,9},{9,10},{10,1... | collective-permute-start | bytes 6291464 | tf_op jit(solution)/shard_map/ppermute | solution.py:14
  (127 other events, 542.0 us)
where the time goes:
time: 529 us; the launch traced here: 520 us
  local copies, waits for them, and re-layouts  244 us (46%)
  matrix products  112 us (21%)
  blocking collectives  47.9 us (9%)
  between operations  47.5 us (9%)
  other arithmetic  36.1 us (7%)
  starting transfers between devices  32.2 us (6%)
    gather x46, local copies, waits for them, and re-layouts, couple(): picked = window[positions[:, slot_idx]]  93.8 us
    unnamed x403, local copies, waits for them, and re-layouts  92.3 us
    dot_general x68, matrix products, couple(): jnp.einsum('mrs,msv->mrv', blocks[:, slot_idx], picked, preferred_element...  77.2 us
    all_gather x1, blocking collectives, shards(): gathered = lax.all_gather(root_term[None], 'leaf', axis=0, tiled=True)  47.9 us
    ppermute x6, starting transfers between devices, with_halo(): before = lax.ppermute(last, axis, up)  24.1 us
    squeeze x9, local copies, waits for them, and re-layouts, couple(): blocks[:, slot_idx]  23.5 us
    slice x5, local copies, waits for them, and re-layouts, couple(): blocks[:, slot_idx]  16.6 us
    gather x30, other arithmetic, couple(): picked = window[positions[:, slot_idx]]  16.5 us
  transfers between devices with their start and end apart: 12, of which 0 were waited for; matrix products, arithmetic and copies ran while one was open for 59% of the time, Pallas kernels for 0%

commit v1 on v0

v1 whole, which is shorter than its diff:
```python
import functools

import jax
import jax.numpy as jnp
from jax import lax
from jax.experimental import pallas as pl
from jax.experimental.pallas import tpu as pltpu
from jax.sharding import PartitionSpec as P

BF = jnp.bfloat16
F32 = jnp.float32
VMEM = pl.BlockSpec(memory_space=pltpu.VMEM)
SMEM = pl.BlockSpec(memory_space=pltpu.SMEM)
PARAMS = pltpu.CompilerParams(vmem_limit_bytes=56 * 1024 * 1024)


def mask_of(rows, cols, row_block, col_block):
    row = lax.broadcasted_iota(jnp.int32, (rows, cols), 0) // row_block
    col = lax.broadcasted_iota(jnp.int32, (rows, cols), 1) // col_block
    return jnp.where(row == col, 1.0, 0.0).astype(BF)


def dot(a, b):
    return jnp.dot(a, b, preferred_element_type=F32)


def rows_at(start, size):
    if isinstance(start, int):
        return pl.ds(start, size)
    return pl.ds(pl.multiple_of(start, 32), size)


def spread(group, mask):
    return jnp.concatenate([group] * 4, axis=0) * mask


def up_pass(x_ref, g_ref, dst_ref, level_rows, rank, leaf_dev, lowest):
    mask = mask_of(4 * rank, 256, rank, 64)
    depth = leaf_dev.bit_length() - 1
    groups = leaf_dev // 4

    def leaves(i, carry):
        out = dot(spread(g_ref[i], mask), x_ref[rows_at(i * 256, 256), :])
        dst_ref[rows_at(level_rows[depth] + i * 128, 128), :] = out.astype(BF)
        return carry

    lax.fori_loop(0, groups, leaves, 0, unroll=4)
    for k in range(depth - 1, lowest - 1, -1):
        count = 2**k // 4
        base = groups + 2 ** (k + 1) // 8 - 2

        def nodes(i, carry, k=k, base=base):
            src = dst_ref[rows_at(level_rows[k + 1] + i * 256, 256), :]
            out = dot(spread(g_ref[base + i], mask), src)
            dst_ref[rows_at(level_rows[k] + i * 128, 128), :] = out.astype(BF)
            return carry

        lax.fori_loop(0, count, nodes, 0, unroll=min(4, count))


def own_kernel(rank, leaf_dev, x_ref, g_ref, low_ref, coeff_ref, root_ref):
    depth = leaf_dev.bit_length() - 1
    level_rows = {k: (2**k - 8) * rank for k in range(3, depth + 1)}
    up_pass(x_ref, g_ref, coeff_ref, level_rows, rank, leaf_dev, 3)
    mask = mask_of(4 * rank, 256, rank, 64)
    state = coeff_ref[0:256, :]
    zeros = jnp.zeros((128, state.shape[1]), BF)
    for step in range(4):
        out = dot(spread(low_ref[step], mask), state)
        if step < 3:
            state = jnp.concatenate([out.astype(BF), zeros], axis=0)
    root_ref[...] = out[0:rank, :]


def top_kernel(rank, top_depth, pos_ref, g_ref, up_ref, s_ref, e_ref, low_ref, out_ref, win):
    up_mask = mask_of(4 * rank, 256, rank, 64)
    count = 2 ** (top_depth - 1)
    for i in range(count):
        pair = g_ref[2 * i * rank : (2 * i + 1) * rank, :]
        other = g_ref[(2 * i + 1) * rank : (2 * i + 2) * rank, :]
        win[(count + i) * rank : (count + i + 1) * rank, :] = (pair + other).astype(BF)
    for k in range(top_depth - 2, 1, -1):
        for i in range(2**k // 4):
            src = win[(2 ** (k + 1)) * rank + i * 256 : (2 ** (k + 1)) * rank + (i + 1) * 256, :]
            out = dot(spread(up_ref[2 ** (k + 1) // 8 - 1 + i], up_mask), src)
            win[2**k * rank + i * 128 : 2**k * rank + (i + 1) * 128, :] = out.astype(BF)
    win[0:rank, :] = jnp.zeros((rank, win.shape[1]), BF)
    carried = None
    slots = s_ref.shape[2] // rank
    for j in range(top_depth - 2):
        parts = [
            win[rows_at(pos_ref[j * slots + s] * rank, rank), :] for s in range(slots)
        ]
        far = dot(s_ref[j], jnp.concatenate(parts, axis=0))
        if carried is not None:
            far = far + dot(e_ref[j], carried)
        carried = far.astype(BF)
    state = dot(low_ref[0:rank, 0:rank], carried).astype(BF)
    first = dot(low_ref[rank : 3 * rank, 0:rank], state).astype(BF)
    halves = [
        dot(low_ref[(3 + 2 * i) * rank : (5 + 2 * i) * rank, 0:rank], first[i * rank : (i + 1) * rank])
        for i in range(2)
    ]
    out_ref[...] = jnp.concatenate(halves, axis=0).astype(BF)


def near_kernel(leaf_dev, size, pos_ref, b_ref, xb_ref, xo_ref, xa_ref, out_ref, win, sems):
    copies = []
    rows = leaf_dev * size
    for i, src in enumerate((xb_ref, xo_ref, xa_ref)):
        copies.append(pltpu.make_async_copy(src, win.at[pl.ds(i * rows, rows)], sems.at[i]))
        copies[-1].start()
    win[3 * rows : 3 * rows + size, :] = jnp.zeros((size, win.shape[1]), BF)
    for copy in copies:
        copy.wait()
    slots = b_ref.shape[2] // size

    def leaf(l, carry):
        parts = [
            win[pl.ds(pl.multiple_of(pos_ref[l * slots + s] * size, size), size), :]
            for s in range(slots)
        ]
        out_ref[pl.ds(pl.multiple_of(l * size, size), size), :] = dot(
            b_ref[l], jnp.concatenate(parts, axis=0)
        )
        return carry

    lax.fori_loop(0, leaf_dev, leaf, 0, unroll=4)


def far_kernel(
    rank,
    leaf_dev,
    pos_ref,
    xb_ref,
    xa_ref,
    gb_ref,
    ga_ref,
    coeff_ref,
    s_ref,
    e_ref,
    basis_ref,
    down_ref,
    near_ref,
    out_ref,
    win,
    down,
):
    depth = leaf_dev.bit_length() - 1
    offset = {k: 3 * (2**k - 8) * rank for k in range(3, depth + 1)}
    for k in range(3, depth + 1):
        size = 2**k * rank
        win[offset[k] + size : offset[k] + 2 * size, :] = coeff_ref[
            (2**k - 8) * rank : (2**k - 8) * rank + size, :
        ]
    total = 3 * (2 ** (depth + 1) - 8) * rank
    win[total : total + rank, :] = jnp.zeros((rank, win.shape[1]), BF)
    up_pass(xb_ref, gb_ref, win, offset, rank, leaf_dev, 3)
    after = {k: offset[k] + 2 * 2**k * rank for k in offset}
    up_pass(xa_ref, ga_ref, win, after, rank, leaf_dev, 3)
    mask = mask_of(256, 128, 64, 32)
    slots = s_ref.shape[2] // rank
    down[0:128, :] = down_ref[...]
    for k in range(3, depth + 1):

        def group(i, carry, k=k):
            parents = down[rows_at((2 ** (k - 1) - 4) * rank + i * 128, 128), :]
            base = (2**k - 8) + i * 8
            total_now = dot(e_ref[rows_at(base * rank, 256), :] * mask, parents)
            fars = []
            for j in range(8):
                node = base + j
                parts = [
                    win[rows_at(pos_ref[node * slots + s] * rank, rank), :] for s in range(slots)
                ]
                fars.append(dot(s_ref[node], jnp.concatenate(parts, axis=0)))
            total_now = total_now + jnp.concatenate(fars, axis=0)
            down[rows_at((2**k - 4) * rank + i * 256, 256), :] = total_now.astype(BF)
            return carry

        lax.fori_loop(0, 2**k // 8, group, 0)

    def leaves(i, carry):
        state = down[rows_at((2**depth - 4) * rank + i * 128, 128), :]
        here = rows_at(i * 256, 256)
        out = near_ref[here, :] + dot(basis_ref[here, :] * mask, state)
        out_ref[here, :] = out.astype(BF)
        return carry

    lax.fori_loop(0, leaf_dev // 4, leaves, 0, unroll=2)


def grouped_up(transfer):
    count, rank = transfer.shape[0], transfer.shape[1]
    return transfer.reshape(count // 8, 8, rank, rank).transpose(0, 3, 1, 2).reshape(-1, rank, 8 * rank)


def shards(
    points,
    leaf_basis,
    local_transfer,
    top_transfer,
    local_coupling,
    local_lists,
    top_coupling,
    top_lists,
    near_blocks,
    near_lists,
):
    leaf_dev, size, rank = leaf_basis.shape
    vecs = points.shape[1]
    depth = leaf_dev.bit_length() - 1
    devices = lax.axis_size("leaf")
    top_depth = devices.bit_length() - 1
    own = lax.axis_index("leaf")
    up = [(i, i + 1) for i in range(devices - 1)]
    back = [(i + 1, i) for i in range(devices - 1)]

    x_before = lax.ppermute(points, "leaf", up)
    x_after = lax.ppermute(points, "leaf", back)
    basis_up = (
        leaf_basis.reshape(leaf_dev // 4, 4, size, rank)
        .transpose(0, 3, 1, 2)
        .reshape(leaf_dev // 4, rank, 4 * size)
    )
    g_own = jnp.concatenate([basis_up, grouped_up(local_transfer[15:])], axis=0)
    g_before = lax.ppermute(g_own, "leaf", up)
    g_after = lax.ppermute(g_own, "leaf", back)

    def padded(rows):
        flat = rows.transpose(2, 0, 1).reshape(rank, -1)
        return jnp.pad(flat, ((0, 0), (0, 256 - flat.shape[1])))

    low_up = jnp.stack(
        [padded(local_transfer[a:b]) for a, b in ((7, 15), (3, 7), (1, 3), (0, 1))]
    )
    nodes = 2 * leaf_dev - 8
    coeff_own, root_term = pl.pallas_call(
        functools.partial(own_kernel, rank, leaf_dev),
        out_shape=(
            jax.ShapeDtypeStruct((nodes * rank, vecs), BF),
            jax.ShapeDtypeStruct((rank, vecs), F32),
        ),
        in_specs=[VMEM] * 3,
        out_specs=(VMEM, VMEM),
        compiler_params=PARAMS,
        cost_estimate=pl.CostEstimate(flops=600_000_000, bytes_accessed=5_000_000, transcendentals=0),
        name="own_up",
    )(points, g_own, low_up)
    gathered = lax.all_gather(root_term, "leaf", axis=0, tiled=True)

    steps = jnp.arange(2, top_depth)
    ancestors = (devices + own) >> (top_depth - steps)
    lists = top_lists[ancestors]
    top_pos = jnp.where(lists >= 0, lists, 0).reshape(-1)
    s_top = top_coupling[ancestors].transpose(0, 2, 1, 3).reshape(top_depth - 2, rank, -1)
    e_top = top_transfer[ancestors]
    low_down = local_transfer[:8].reshape(8 * rank, rank)
    down_two = pl.pallas_call(
        functools.partial(top_kernel, rank, top_depth),
        out_shape=jax.ShapeDtypeStruct((4 * rank, vecs), BF),
        in_specs=[SMEM] + [VMEM] * 5,
        out_specs=VMEM,
        scratch_shapes=[pltpu.VMEM((devices * rank, vecs), BF)],
        compiler_params=PARAMS,
        cost_estimate=pl.CostEstimate(flops=50_000_000, bytes_accessed=1_000_000, transcendentals=0),
        name="top_tree",
    )(top_pos, gathered, grouped_up(top_transfer[8:]), s_top, e_top, low_down)

    first_leaf = (own - 1) * leaf_dev
    near_pos = jnp.where(near_lists >= 0, near_lists - first_leaf, 3 * leaf_dev).reshape(-1)
    near_cat = near_blocks.transpose(0, 2, 1, 3).reshape(leaf_dev, size, -1)
    near_rows = pl.pallas_call(
        functools.partial(near_kernel, leaf_dev, size),
        out_shape=jax.ShapeDtypeStruct((leaf_dev * size, vecs), F32),
        in_specs=[SMEM, VMEM] + [pl.BlockSpec(memory_space=pl.ANY)] * 3,
        out_specs=VMEM,
        scratch_shapes=[
            pltpu.VMEM(((3 * leaf_dev + 1) * size, vecs), BF),
            pltpu.SemaphoreType.DMA((3,)),
        ],
        compiler_params=PARAMS,
        cost_estimate=pl.CostEstimate(
            flops=2_000_000_000, bytes_accessed=20_000_000, transcendentals=0
        ),
        name="near_field",
    )(near_pos, near_cat, x_before, points, x_after)

    far_lists = local_lists[7:]
    row = jnp.arange(7, 2 * leaf_dev - 1)
    width = jnp.zeros_like(row)
    for k in range(3, depth + 1):
        width = jnp.where(row >= 2**k - 1, 2**k, width)
    start = 3 * (width - 8) - (own - 1) * width
    far_pos = jnp.where(far_lists >= 0, far_lists + start[:, None], 3 * nodes).reshape(-1)
    s_cat = local_coupling[7:].transpose(0, 2, 1, 3).reshape(nodes, rank, -1)
    e_tiled = jnp.tile(local_transfer[7:], (1, 1, 4)).reshape(nodes * rank, 4 * rank)
    basis_tiled = jnp.tile(leaf_basis, (1, 1, 4)).reshape(leaf_dev * size, 4 * rank)
    return pl.pallas_call(
        functools.partial(far_kernel, rank, leaf_dev),
        out_shape=jax.ShapeDtypeStruct((leaf_dev * size, vecs), BF),
        in_specs=[SMEM] + [VMEM] * 10,
        out_specs=VMEM,
        scratch_shapes=[
            pltpu.VMEM(((3 * nodes + 1) * rank, vecs), BF),
            pltpu.VMEM(((nodes + 4) * rank, vecs), BF),
        ],
        compiler_params=PARAMS,
        cost_estimate=pl.CostEstimate(
            flops=2_000_000_000, bytes_accessed=20_000_000, transcendentals=0
        ),
        name="far_field",
    )(
        far_pos,
        x_before,
        x_after,
        g_before,
        g_after,
        coeff_own,
        s_cat,
        e_tiled,
        basis_tiled,
        down_two,
        near_rows,
    )


def solution(mesh):
    return jax.shard_map(
        shards,
        mesh=mesh,
        in_specs=(
            P("leaf", None),
            P("leaf", None, None),
            P("leaf", None, None),
            P(),
            P("leaf", None, None, None),
            P("leaf", None),
            P(),
            P(),
            P("leaf", None, None, None),
            P("leaf", None),
        ),
        out_specs=P("leaf", None),
        check_vma=False,
    )
```

time: 529 us -> 210 us (0.40); the launches traced: 520 us -> 209 us
  local copies, waits for them, and re-layouts: 244 us -> 87.7 us
  matrix products: 112 us -> 0 us
  Pallas kernels: 0 us -> 58.5 us
  between operations: 47.5 us -> 0.21 us
  other arithmetic: 36.1 us -> 3.36 us
  starting transfers between devices: 32.2 us -> 11.3 us
    dot_general x88 -> x0, matrix products: 112 us -> none  [the longest x68 77.2 us: couple(): jnp.einsum('mrs,msv->mrv', blocks[:, slot_idx], picked, preferred_element...]
    gather x46 -> x4, local copies, waits for them, and re-layouts: 93.8 us -> 3.33 us  [the longest x1 2.11 us: shards(): e_top = top_transfer[ancestors]]
    unnamed x403 -> x30, local copies, waits for them, and re-layouts: 92.3 us -> 15.3 us
    pallas_call x0 -> x4, Pallas kernels: none -> 58.5 us  [the longest x1 31.4 us: shards(): pl.pallas_call(functools.partial(far_kernel, rank, leaf_dev), out_shape=j...]
    another operation x0 -> x9, local copies, waits for them, and re-layouts: none -> 26.6 us  [the longest x3 15.3 us: shards(): jnp.tile(local_transfer[7:], (1, 1, 4)).reshape(nodes * rank, 4 * rank)]
    slice x18 -> x9, local copies, waits for them, and re-layouts: 30.9 us -> 5.18 us  [the longest x2 2.13 us: shards(): local_transfer[7:]]
    reshape x0 -> x11, local copies, waits for them, and re-layouts: none -> 24.7 us  [the longest x1 9.05 us: shards(): near_cat = near_blocks.transpose(0, 2, 1, 3).reshape(leaf_dev, size, -1)]
    squeeze x9 -> x0, local copies, waits for them, and re-layouts: 23.5 us -> none  [couple(): blocks[:, slot_idx]]
  transfers between devices with their start and end apart: 12 -> 4, of which waited for: 0 -> 0; matrix products, arithmetic and copies ran while one was open for 59% -> 44% of each run, Pallas kernels for 0% -> 13%
where the time goes in v1:
time: 210 us; the launch traced here: 209 us
  local copies, waits for them, and re-layouts  87.7 us (42%)
  Pallas kernels  58.5 us (28%)
  blocking collectives  47.6 us (23%)
  starting transfers between devices  11.3 us (5%)
  other arithmetic  3.36 us (2%)
    all_gather x1, blocking collectives, shards(): gathered = lax.all_gather(root_term, 'leaf', axis=0, tiled=True)  47.6 us
    pallas_call x1, Pallas kernels, shards(): pl.pallas_call(functools.partial(far_kernel, rank, leaf_dev), out_shape=j...  31.4 us
    another operation x3, local copies, waits for them, and re-layouts, shards(): jnp.tile(local_transfer[7:], (1, 1, 4)).reshape(nodes * rank, 4 * rank)  15.3 us
    unnamed x30, local copies, waits for them, and re-layouts  15.3 us
    pallas_call x1, Pallas kernels, shards(): pl.pallas_call(functools.partial(near_kernel, leaf_dev, size), out_shape=...  14.8 us
    another operation x3, local copies, waits for them, and re-layouts, shards(): jnp.tile(leaf_basis, (1, 1, 4)).reshape(leaf_dev * size, 4 * rank)  11.2 us
    pallas_call x1, Pallas kernels, shards(): pl.pallas_call(functools.partial(own_kernel, rank, leaf_dev), out_shape=(...  9.42 us
    reshape x1, local copies, waits for them, and re-layouts, shards(): near_cat = near_blocks.transpose(0, 2, 1, 3).reshape(leaf_dev, size, -1)  9.05 us
  transfers between devices with their start and end apart: 4, of which 0 were waited for; matrix products, arithmetic and copies ran while one was open for 44% of the time, Pallas kernels for 13%

profile of v1, /device:TPU:0, one launch (start us, length us, event | category | flops | bytes accessed | tf_op | source)
XLA Modules:
  0.0 208.7 jit_solution(14165910777381337134)
XLA Ops:
  0.0 0.0 copy-start
  0.0 3.8 %collective-permute-start = (bf16[8192,128]{1,0:T(8,128)(2,1)}, bf16[8192,128]{1,0:T(8,128)(2,1)}, u32[]{:S(2)}, u32[]{:S(2)}) collective-permute-start(bf16[8192,128]{1,0:T(8,128)(2,1)} %xo_ref.1), channel_id=1, source_target_pairs={{0,1},{1,2},{2,3},{3,4},{4,5},{5,6},{6,7},{7,8},{8,9},{9,10},{10,1... | collective-permute-start | bytes 6291464 | tf_op jit(solution)/shard_map/ppermute | solution.py:219
  3.8 1.3 collective-permute-start.1
  5.1 1.3 slice.31
  6.4 2.6 %copy.48 = bf16[240,32,32]{2,1,0:T(8,128)(2,1)} copy(bf16[240,32,32]{0,2,1:T(8,128)(2,1)S(1)} %slice.31) | data formatting | bytes 983040
  9.0 2.5 %copy.47 = bf16[30,32,256]{2,1,0:T(8,128)(2,1)} copy(bf16[30,32,256]{1,2,0:T(8,128)(2,1)} %bitcast.49) | data formatting | bytes 983040 | tf_op jit(solution)/shard_map/reshape | solution.py:195
  11.6 2.8 %copy.26 = bf16[128,64,32]{1,2,0:T(8,128)(2,1)S(1)} copy(bf16[128,64,32]{0,2,1:T(8,128)(2,1)} %param.11) | data formatting | bytes 1048576 | tf_op args[1]
  14.4 1.5 copy.27
  15.9 2.1 %reshape.99 = bf16[32,32,256]{2,1,0:T(8,128)(2,1)S(1)} reshape(bf16[32,32,4,64]{3,2,1,0:T(4,128)(2,1)} %copy.27) | data formatting | bytes 1048576 | tf_op jit(solution)/shard_map/reshape | solution.py:224
  18.1 2.1 %pad_maximum_fusion.g_ref = bf16[62,32,256]{2,1,0:T(8,128)(2,1)} fusion(bf16[30,32,256]{2,1,0:T(8,128)(2,1)} %copy.47, bf16[32,32,256]{2,1,0:T(8,128)(2,1)S(1)} %reshape.99), kind=kLoop, calls=%fused_computation.4 | loop fusion | flops 507904 | bytes 2031616 | tf_op jit(solution)/shard_map/concatenate | solution.py:226
  20.2 4.9 %collective-permute-start.2 = (bf16[62,32,256]{2,1,0:T(8,128)(2,1)}, bf16[62,32,256]{2,1,0:T(8,128)(2,1)}, u32[]{:S(2)}, u32[]{:S(2)}) collective-permute-start(bf16[62,32,256]{2,1,0:T(8,128)(2,1)} %pad_maximum_fusion.g_ref), channel_id=1, source_target_pairs={{0,1},{1,2},{2,3},{3,4},{4,5},{5,6},{6,7},{7,8},{8,9},{9,10},{10,1... | collective-permute-start | bytes 3047432 | tf_op jit(solution)/shard_map/ppermute | solution.py:227
  25.1 1.3 collective-permute-start.3
  26.4 1.0 fusion.1
  27.4 0.8 slice_bitcast_fusion.1
  28.2 0.9 slice_bitcast_fusion.2
  29.1 1.0 slice.37
  30.1 1.6 copy.36
  31.7 1.3 copy.30
  33.0 0.1 stack.15
  33.1 0.4 copy.32
  33.5 0.1 reshape.103
  33.6 0.0 slice-done
  33.6 0.4 copy.49
  34.0 0.4 copy.31
  34.4 0.1 reshape.102
  34.5 2.1 %gather_fusion.2 = bf16[3,32,32]{2,1,0:T(8,128)(2,1)} fusion(bf16[32,32,32]{2,1,0:T(8,128)(2,1)} %param.13, s32[1024]{0:T(1024)S(1)} %pad_clamp_fusion), kind=kCustom, calls=%fused_computation.2 | custom fusion | bytes 12300 | tf_op jit(solution)/shard_map/gather | solution.py:257
  36.6 0.6 gather_fusion.1
  37.2 0.1 copy.39
  37.3 0.8 reshape.108.s_ref
  38.1 0.1 copy.37
  38.2 0.6 gather_fusion
  38.7 0.1 gather.12
  38.8 0.8 copy.40
  39.6 0.2 copy.38
  39.8 0.8 reshape.107.up_ref
  40.6 0.1 copy.41
  40.7 0.7 reshape.110.pos_ref
  41.4 7.7 %copy.42 = bf16[128,6,64,64]{0,3,1,2:T(8,128)(2,1)} copy(bf16[128,6,64,64]{0,3,2,1:T(8,128)(2,1)} %param.18) | data formatting | bytes 12582912 | tf_op args[8]
  49.1 9.0 %copy.43.b_ref = bf16[128,64,384]{2,1,0:T(8,128)(2,1)} copy(bf16[128,64,384]{0,2,1:T(8,128)(2,1)} %bitcast.47) | data formatting | bytes 12582912 | tf_op jit(solution)/shard_map/reshape | solution.py:272
  58.2 0.1 add_select_fusion
  58.3 0.1 copy.25
  58.4 0.7 reshape.97.pos_ref
  59.1 1.1 copy.35
  60.2 4.3 %tile.16 = bf16[248,1,32,4,32]{2,0,4,3,1:T(8,128)(2,1)} broadcast(bf16[248,32,32]{1,0,2:T(8,128)(2,1)S(1)} %copy.35), dimensions={0,2,4} | broadcast | bytes 2539520 | tf_op jit(solution)/shard_map/tile | solution.py:297
  64.5 8.4 %tile.17 = bf16[7936,128]{0,1:T(8,128)(2,1)S(1)} reshape(bf16[248,1,32,4,32]{2,0,4,3,1:T(8,128)(2,1)} %tile.16) | data formatting | bytes 4063232 | tf_op jit(solution)/shard_map/tile | solution.py:297
  73.0 2.5 %copy.45.e_ref = bf16[7936,128]{1,0:T(8,128)(2,1)} copy(bf16[7936,128]{0,1:T(8,128)(2,1)S(1)} %tile.17) | data formatting | bytes 4063232 | tf_op jit(solution)/shard_map/tile | solution.py:297
  75.5 4.6 %slice_bitcast_fusion = bf16[248,32,8,32]{0,3,1,2:T(8,128)(2,1)S(1)} fusion(bf16[255,8,32,32]{0,3,2,1:T(8,128)(2,1)} %param.14), kind=kLoop, calls=%fused_computation.3 | loop fusion | bytes 8126464 | tf_op jit(solution)/shard_map/transpose | solution.py:296
  80.1 2.4 %copy.34 = bf16[248,32,8,32]{0,3,2,1:T(8,128)(2,1)} copy(bf16[248,32,8,32]{0,3,1,2:T(8,128)(2,1)S(1)} %slice_bitcast_fusion) | data formatting | bytes 8126464 | tf_op jit(solution)/shard_map/transpose | solution.py:296
  82.5 7.6 %copy.44.s_ref = bf16[248,32,256]{2,1,0:T(8,128)(2,1)} copy(bf16[248,32,256]{0,2,1:T(8,128)(2,1)} %bitcast.48) | data formatting | bytes 8126464 | tf_op jit(solution)/shard_map/reshape | solution.py:296
  90.2 3.1 %tile.18 = bf16[128,1,64,4,32]{2,0,4,3,1:T(8,128)(2,1)} broadcast(bf16[128,64,32]{1,0,2:T(8,128)(2,1)S(1)} %copy-done.3), dimensions={0,2,4} | broadcast | bytes 2621440 | tf_op jit(solution)/shard_map/tile | solution.py:298
  93.2 5.7 %tile.19 = bf16[8192,128]{0,1:T(8,128)(2,1)S(1)} reshape(bf16[128,1,64,4,32]{2,0,4,3,1:T(8,128)(2,1)} %tile.18) | data formatting | bytes 4194304 | tf_op jit(solution)/shard_map/tile | solution.py:298
  98.9 2.5 %copy.46.basis_ref = bf16[8192,128]{1,0:T(8,128)(2,1)} copy(bf16[8192,128]{0,1:T(8,128)(2,1)S(1)} %tile.19) | data formatting | bytes 4194304 | tf_op jit(solution)/shard_map/tile | solution.py:298
  101.4 0.6 pad_maximum_fusion.1.low_ref
  102.0 9.4 %own_up.1 = (bf16[7936,128]{1,0:T(8,128)(2,1)}, f32[32,128]{1,0:T(8,128)}) custom-call(bf16[8192,128]{1,0:T(8,128)(2,1)} %xo_ref.1, bf16[62,32,256]{2,1,0:T(8,128)(2,1)} %pad_maximum_fusion.g_ref, bf16[4,32,256]{2,1,0:T(8,128)(2,1)} %pad_maximum_fusion.1.low_ref), custom_call_target="tpu_custom_call" | custom-call | flops 600000000 | bytes 5000000 | tf_op jit(solution)/shard_map/own_up/pallas_call | solution.py:238
  111.4 0.5 compare_select_fusion.pos_ref
  111.9 47.6 %all_gather.3.g_ref = f32[1024,128]{1,0:T(8,128)} all-gather(f32[32,128]{1,0:T(8,128)} %get-tuple-element.8), channel_id=1, replica_groups=mesh['leaf'=32] {'leaf'}, dimensions={0}, use_global_device_ids=true | all-gather | bytes 540672 | tf_op jit(solution)/shard_map/all_gather | solution.py:250
  159.5 2.9 %top_tree.1.down_ref = bf16[128,128]{1,0:T(8,128)(2,1)} custom-call(s32[24]{0:T(128)} %compare_select_fusion.pos_ref, f32[1024,128]{1,0:T(8,128)} %all_gather.3.g_ref, bf16[3,32,256]{2,1,0:T(8,128)(2,1)} %reshape.107.up_ref, bf16[3,32,256]{2,1,0:T(8,128)(2,1)} %reshape.108.s_ref, bf16[3,32,32]{2,1,0:T(8,128)(2,1)} %gather_fusion.2, bf16[256,32]{1,0:T(8,128)(2,1)} %bitcast.54), custom_call_target="tpu_custom_call" | custom-call | flops 50000000 | bytes 1000000 | tf_op jit(solution)/shard_map/top_tree/pallas_call | solution.py:259
  162.4 0.0 collective-permute-done.xb_ref
  162.4 0.0 collective-permute-done.1.xa_ref
  162.4 14.8 %near_field.1.near_ref = f32[8192,128]{1,0:T(8,128)} custom-call(s32[768]{0:T(1024)} %reshape.110.pos_ref, bf16[128,64,384]{2,1,0:T(8,128)(2,1)} %copy.43.b_ref, bf16[8192,128]{1,0:T(8,128)(2,1)} %collective-permute-done.xb_ref, bf16[8192,128]{1,0:T(8,128)(2,1)} %xo_ref.1, bf16[8192,128]{1,0:T(8,128)(2,1)} %collective-permute-done.1.xa_ref), custom_call_target="tpu_custom_call" | custom-call | flops 2000000000 | bytes 20000000 | tf_op jit(solution)/shard_map/near_field/pallas_call | solution.py:273
  177.2 0.0 collective-permute-done.2.gb_ref
  177.2 0.0 collective-permute-done.3.ga_ref
  177.2 0.0 copy-start.1
  177.2 31.4 %far_field.1 = bf16[8192,128]{1,0:T(8,128)(2,1)} custom-call(s32[1984]{0:T(1024)} %reshape.97.pos_ref, bf16[8192,128]{1,0:T(8,128)(2,1)} %collective-permute-done.xb_ref, bf16[8192,128]{1,0:T(8,128)(2,1)} %collective-permute-done.1.xa_ref, bf16[62,32,256]{2,1,0:T(8,128)(2,1)} %collective-permute-done.2.gb_ref, ...), custom_call_target="tpu_custom_call" | custom-call | flops 2000000000 | bytes 20000000 | tf_op jit(solution)/shard_map/far_field/pallas_call | solution.py:299
  (31 shorter events, 0.1 us)
Async XLA Ops:
  0.0 36.6 %copy-start = (bf16[32,8,32,32]{3,2,1,0:T(8,128)(2,1)S(1)}, bf16[32,8,32,32]{3,2,1,0:T(8,128)(2,1)}, u32[]{:S(2)}) copy-start(bf16[32,8,32,32]{3,2,1,0:T(8,128)(2,1)} %param.16) | copy-start | bytes 1572868
  0.0 162.4 %collective-permute-start = (bf16[8192,128]{1,0:T(8,128)(2,1)}, bf16[8192,128]{1,0:T(8,128)(2,1)}, u32[]{:S(2)}, u32[]{:S(2)}) collective-permute-start(bf16[8192,128]{1,0:T(8,128)(2,1)} %xo_ref.1), channel_id=1, source_target_pairs={{0,1},{1,2},{2,3},{3,4},{4,5},{5,6},{6,7},{7,8},{8,9},{9,10},{10,1... | collective-permute-start | bytes 6291464 | tf_op jit(solution)/shard_map/ppermute | solution.py:219
  3.8 158.6 %collective-permute-start.1 = (bf16[8192,128]{1,0:T(8,128)(2,1)}, bf16[8192,128]{1,0:T(8,128)(2,1)}, u32[]{:S(2)}, u32[]{:S(2)}) collective-permute-start(bf16[8192,128]{1,0:T(8,128)(2,1)} %xo_ref.1), channel_id=1, source_target_pairs={{1,0},{2,1},{3,2},{4,3},{5,4},{6,5},{7,6},{8,7},{9,8},{10,9},{11,1... | collective-permute-start | bytes 6291464 | tf_op jit(solution)/shard_map/ppermute | solution.py:220
  15.9 10.5 %copy-start.2 = (bf16[255,32,32]{0,2,1:T(8,128)(2,1)S(1)}, bf16[255,32,32]{0,2,1:T(8,128)(2,1)}, u32[]{:S(2)}) copy-start(bf16[255,32,32]{0,2,1:T(8,128)(2,1)} %param.12) | copy-start | bytes 1566724
  20.2 9.9 %copy-start.4 = (bf16[128,64,32]{0,2,1:T(8,128)(2,1)S(1)}, bf16[128,64,32]{0,2,1:T(8,128)(2,1)}, u32[]{:S(2)}) copy-start(bf16[128,64,32]{0,2,1:T(8,128)(2,1)} %param.11) | copy-start | bytes 1572868
  20.2 157.0 %collective-permute-start.2 = (bf16[62,32,256]{2,1,0:T(8,128)(2,1)}, bf16[62,32,256]{2,1,0:T(8,128)(2,1)}, u32[]{:S(2)}, u32[]{:S(2)}) collective-permute-start(bf16[62,32,256]{2,1,0:T(8,128)(2,1)} %pad_maximum_fusion.g_ref), channel_id=1, source_target_pairs={{0,1},{1,2},{2,3},{3,4},{4,5},{5,6},{6,7},{7,8},{8,9},{9,10},{10,1... | collective-permute-start | bytes 3047432 | tf_op jit(solution)/shard_map/ppermute | solution.py:227
  25.1 152.1 %collective-permute-start.3 = (bf16[62,32,256]{2,1,0:T(8,128)(2,1)}, bf16[62,32,256]{2,1,0:T(8,128)(2,1)}, u32[]{:S(2)}, u32[]{:S(2)}) collective-permute-start(bf16[62,32,256]{2,1,0:T(8,128)(2,1)} %pad_maximum_fusion.g_ref), channel_id=1, source_target_pairs={{1,0},{2,1},{3,2},{4,3},{5,4},{6,5},{7,6},{8,7},{9,8},{10,9},{11,1... | collective-permute-start | bytes 3047432 | tf_op jit(solution)/shard_map/ppermute | solution.py:228
  28.2 5.4 %slice-start = ((bf16[255,32,32]{0,2,1:T(8,128)(2,1)}), bf16[1,32,32]{0,2,1:T(8,128)(2,1)S(1)}, s32[]{:S(2)}) async-start(bf16[255,32,32]{0,2,1:T(8,128)(2,1)} %param.12), calls=%async_computation | async-start | bytes 524288 | tf_op jit(solution)/shard_map/slice | solution.py:235
  30.1 3.0 %copy-start.7 = (bf16[32,2,32]{1,0,2:T(8,128)(2,1)S(1)}, bf16[32,2,32]{1,0,2:T(8,128)(2,1)}, u32[]{:S(2)}) copy-start(bf16[32,2,32]{1,0,2:T(8,128)(2,1)} %slice_bitcast_fusion.1) | copy-start | bytes 12292
  30.1 3.9 %copy-start.6 = (bf16[32,4,32]{1,0,2:T(8,128)(2,1)S(1)}, bf16[32,4,32]{1,0,2:T(8,128)(2,1)}, u32[]{:S(2)}) copy-start(bf16[32,4,32]{1,0,2:T(8,128)(2,1)} %slice_bitcast_fusion.2) | copy-start | bytes 24580
  30.1 8.0 %copy-start.10 = (s32[32,8]{0,1:T(8,128)S(1)}, s32[32,8]{0,1:T(8,128)}, u32[]{:S(2)}) copy-start(s32[32,8]{0,1:T(8,128)} %param.17) | copy-start | bytes 3076
  31.7 7.1 %copy-start.8 = (bf16[8,32,32]{0,2,1:T(8,128)(2,1)S(1)}, bf16[8,32,32]{0,2,1:T(8,128)(2,1)}, u32[]{:S(2)}) copy-start(bf16[8,32,32]{0,2,1:T(8,128)(2,1)} %get-tuple-element.9) | copy-start | bytes 49156
  31.7 7.9 %slice-start.1 = ((bf16[32,32,32]{2,1,0:T(8,128)(2,1)}), bf16[24,32,32]{2,1,0:T(8,128)(2,1)S(1)}, s32[]{:S(2)}) async-start(bf16[32,32,32]{2,1,0:T(8,128)(2,1)} %param.13), calls=%async_computation.1 | async-start | bytes 393216 | tf_op jit(solution)/shard_map/slice | solution.py:268
  31.7 8.8 %copy-start.11 = (s32[128,6]{0,1:T(8,128)S(1)}, s32[128,6]{0,1:T(8,128)}, u32[]{:S(2)}) copy-start(s32[128,6]{0,1:T(8,128)} %param.19) | copy-start | bytes 9220
  49.1 9.1 %copy-start.9 = (s32[255,8]{0,1:T(8,128)S(1)}, s32[255,8]{0,1:T(8,128)}, u32[]{:S(2)}) copy-start(s32[255,8]{0,1:T(8,128)} %param.15) | copy-start | bytes 24484
  49.1 10.0 %copy-start.5 = (bf16[248,32,32]{0,2,1:T(8,128)(2,1)S(1)}, bf16[248,32,32]{0,2,1:T(8,128)(2,1)}, u32[]{:S(2)}) copy-start(bf16[248,32,32]{0,2,1:T(8,128)(2,1)} %slice.37) | copy-start | bytes 1523716
  82.5 7.6 %copy-start.3 = (bf16[128,64,32]{1,0,2:T(8,128)(2,1)S(1)}, bf16[128,64,32]{1,0,2:T(8,128)(2,1)}, u32[]{:S(2)}) copy-start(bf16[128,64,32]{1,0,2:T(8,128)(2,1)} %copy.36) | copy-start | bytes 1572868
  177.2 31.4 %copy-start.1 = (bf16[32,8,32,32]{3,2,1,0:T(8,128)(2,1)S(1)}, bf16[32,8,32,32]{3,2,1,0:T(8,128)(2,1)}, u32[]{:S(2)}) copy-start(bf16[32,8,32,32]{3,2,1,0:T(8,128)(2,1)} %param.16) | copy-start | bytes 1572868

commit v2 on v1

--- a/solution.py
+++ b/solution.py
@@ -34,25 +34,27 @@
     return jnp.concatenate([group] * 4, axis=0) * mask
 
 
-def up_pass(x_ref, g_ref, dst_ref, level_rows, rank, leaf_dev, lowest):
+def up_pass(sides, dst_ref, rank, leaf_dev):
     mask = mask_of(4 * rank, 256, rank, 64)
     depth = leaf_dev.bit_length() - 1
     groups = leaf_dev // 4
 
     def leaves(i, carry):
-        out = dot(spread(g_ref[i], mask), x_ref[rows_at(i * 256, 256), :])
-        dst_ref[rows_at(level_rows[depth] + i * 128, 128), :] = out.astype(BF)
+        for x_ref, first, g_ref, level_rows in sides:
+            out = dot(spread(g_ref[i], mask), x_ref[rows_at(first + i * 256, 256), :])
+            dst_ref[rows_at(level_rows[depth] + i * 128, 128), :] = out.astype(BF)
         return carry
 
     lax.fori_loop(0, groups, leaves, 0, unroll=4)
-    for k in range(depth - 1, lowest - 1, -1):
+    for k in range(depth - 1, 2, -1):
         count = 2**k // 4
         base = groups + 2 ** (k + 1) // 8 - 2
 
         def nodes(i, carry, k=k, base=base):
-            src = dst_ref[rows_at(level_rows[k + 1] + i * 256, 256), :]
-            out = dot(spread(g_ref[base + i], mask), src)
-            dst_ref[rows_at(level_rows[k] + i * 128, 128), :] = out.astype(BF)
+            for _, _, g_ref, level_rows in sides:
+                src = dst_ref[rows_at(level_rows[k + 1] + i * 256, 256), :]
+                out = dot(spread(g_ref[base + i], mask), src)
+                dst_ref[rows_at(level_rows[k] + i * 128, 128), :] = out.astype(BF)
             return carry
 
         lax.fori_loop(0, count, nodes, 0, unroll=min(4, count))
@@ -61,7 +63,7 @@
 def own_kernel(rank, leaf_dev, x_ref, g_ref, low_ref, coeff_ref, root_ref):
     depth = leaf_dev.bit_length() - 1
     level_rows = {k: (2**k - 8) * rank for k in range(3, depth + 1)}
-    up_pass(x_ref, g_ref, coeff_ref, level_rows, rank, leaf_dev, 3)
+    up_pass([(x_ref, 0, g_ref, level_rows)], coeff_ref, rank, leaf_dev)
     mask = mask_of(4 * rank, 256, rank, 64)
     state = coeff_ref[0:256, :]
     zeros = jnp.zeros((128, state.shape[1]), BF)
@@ -75,10 +77,7 @@
 def top_kernel(rank, top_depth, pos_ref, g_ref, up_ref, s_ref, e_ref, low_ref, out_ref, win):
     up_mask = mask_of(4 * rank, 256, rank, 64)
     count = 2 ** (top_depth - 1)
-    for i in range(count):
-        pair = g_ref[2 * i * rank : (2 * i + 1) * rank, :]
-        other = g_ref[(2 * i + 1) * rank : (2 * i + 2) * rank, :]
-        win[(count + i) * rank : (count + i + 1) * rank, :] = (pair + other).astype(BF)
+    win[count * rank : 2 * count * rank, :] = g_ref[...]
     for k in range(top_depth - 2, 1, -1):
         for i in range(2**k // 4):
             src = win[(2 ** (k + 1)) * rank + i * 256 : (2 ** (k + 1)) * rank + (i + 1) * 256, :]
@@ -104,74 +103,107 @@
     out_ref[...] = jnp.concatenate(halves, axis=0).astype(BF)
 
 
-def near_kernel(leaf_dev, size, pos_ref, b_ref, xb_ref, xo_ref, xa_ref, out_ref, win, sems):
-    copies = []
-    rows = leaf_dev * size
-    for i, src in enumerate((xb_ref, xo_ref, xa_ref)):
-        copies.append(pltpu.make_async_copy(src, win.at[pl.ds(i * rows, rows)], sems.at[i]))
-        copies[-1].start()
-    win[3 * rows : 3 * rows + size, :] = jnp.zeros((size, win.shape[1]), BF)
-    for copy in copies:
-        copy.wait()
-    slots = b_ref.shape[2] // size
-
-    def leaf(l, carry):
-        parts = [
-            win[pl.ds(pl.multiple_of(pos_ref[l * slots + s] * size, size), size), :]
-            for s in range(slots)
-        ]
-        out_ref[pl.ds(pl.multiple_of(l * size, size), size), :] = dot(
-            b_ref[l], jnp.concatenate(parts, axis=0)
-        )
+def prep_kernel(g_ref, low_ref, e_ref, basis_ref):
+    rank = g_ref.shape[1]
+    mask = mask_of(4 * rank, 256, rank, 64)
+    groups = basis_ref.shape[0] // 256
+
+    def turned(group):
+        return jnp.transpose(spread(group, mask))
+
+    e_ref[0:256, :] = turned(low_ref[0])
+
+    def bases(i, carry):
+        basis_ref[rows_at(i * 256, 256), :] = turned(g_ref[i])
         return carry
 
-    lax.fori_loop(0, leaf_dev, leaf, 0, unroll=4)
-
-
-def far_kernel(
+    def transfers(i, carry):
+        e_ref[rows_at(256 + i * 256, 256), :] = turned(g_ref[groups + i])
+        return carry
+
+    lax.fori_loop(0, groups, bases, 0, unroll=2)
+    lax.fori_loop(0, g_ref.shape[0] - groups, transfers, 0, unroll=2)
+
+
+def field_kernel(
     rank,
     leaf_dev,
-    pos_ref,
-    xb_ref,
-    xa_ref,
-    gb_ref,
-    ga_ref,
-    coeff_ref,
+    size,
+    near_pos,
+    far_pos,
+    xb_hbm,
+    xo_hbm,
+    xa_hbm,
+    gb_hbm,
+    ga_hbm,
+    b_hbm,
+    s_hbm,
+    e_hbm,
+    basis_hbm,
+    coeff_hbm,
+    down_hbm,
+    out_ref,
+    xs,
+    gb,
+    ga,
+    b_ref,
     s_ref,
     e_ref,
     basis_ref,
-    down_ref,
-    near_ref,
-    out_ref,
     win,
     down,
+    sems,
 ):
     depth = leaf_dev.bit_length() - 1
+    rows = leaf_dev * size
     offset = {k: 3 * (2**k - 8) * rank for k in range(3, depth + 1)}
+    copies = []
+
+    def begin(src, dst):
+        copies.append(pltpu.make_async_copy(src, dst, sems.at[len(copies)]))
+        copies[-1].start()
+        return copies[-1]
+
+    first = [
+        begin(gb_hbm, gb),
+        begin(ga_hbm, ga),
+        begin(xb_hbm, xs.at[pl.ds(0, rows)]),
+        begin(xa_hbm, xs.at[pl.ds(2 * rows, rows)]),
+    ]
+    second = [begin(down_hbm, down.at[pl.ds(0, 4 * rank)]), begin(s_hbm, s_ref), begin(e_hbm, e_ref)]
     for k in range(3, depth + 1):
-        size = 2**k * rank
-        win[offset[k] + size : offset[k] + 2 * size, :] = coeff_ref[
-            (2**k - 8) * rank : (2**k - 8) * rank + size, :
-        ]
+        level = 2**k * rank
+        second.append(
+            begin(
+                coeff_hbm.at[pl.ds((2**k - 8) * rank, level)], win.at[pl.ds(offset[k] + level, level)]
+            )
+        )
+    third = [
+        begin(xo_hbm, xs.at[pl.ds(rows, rows)]),
+        begin(basis_hbm, basis_ref),
+        begin(b_hbm, b_ref),
+    ]
     total = 3 * (2 ** (depth + 1) - 8) * rank
     win[total : total + rank, :] = jnp.zeros((rank, win.shape[1]), BF)
-    up_pass(xb_ref, gb_ref, win, offset, rank, leaf_dev, 3)
+    xs[3 * rows : 3 * rows + size, :] = jnp.zeros((size, xs.shape[1]), BF)
+    for copy in first:
+        copy.wait()
     after = {k: offset[k] + 2 * 2**k * rank for k in offset}
-    up_pass(xa_ref, ga_ref, win, after, rank, leaf_dev, 3)
-    mask = mask_of(256, 128, 64, 32)
+    up_pass([(xs, 0, gb, offset), (xs, 2 * rows, ga, after)], win, rank, leaf_dev)
+    for copy in second:
+        copy.wait()
     slots = s_ref.shape[2] // rank
-    down[0:128, :] = down_ref[...]
     for k in range(3, depth + 1):
 
         def group(i, carry, k=k):
             parents = down[rows_at((2 ** (k - 1) - 4) * rank + i * 128, 128), :]
             base = (2**k - 8) + i * 8
-            total_now = dot(e_ref[rows_at(base * rank, 256), :] * mask, parents)
+            total_now = dot(e_ref[rows_at(base * rank, 256), :], parents)
             fars = []
             for j in range(8):
                 node = base + j
                 parts = [
-                    win[rows_at(pos_ref[node * slots + s] * rank, rank), :] for s in range(slots)
+                    win[rows_at(far_pos[node * slots + s] * rank, rank), :] for s in range(slots)
                 ]
                 fars.append(dot(s_ref[node], jnp.concatenate(parts, axis=0)))
             total_now = total_now + jnp.concatenate(fars, axis=0)
@@ -179,11 +211,22 @@
             return carry
 
         lax.fori_loop(0, 2**k // 8, group, 0)
+    for copy in third:
+        copy.wait()
+    near_slots = b_ref.shape[2] // size
 
     def leaves(i, carry):
         state = down[rows_at((2**depth - 4) * rank + i * 128, 128), :]
         here = rows_at(i * 256, 256)
-        out = near_ref[here, :] + dot(basis_ref[here, :] * mask, state)
+        near = []
+        for j in range(4):
+            leaf = i * 4 + j
+            parts = [
+                xs[rows_at(near_pos[leaf * near_slots + s] * size, size), :]
+                for s in range(near_slots)
+            ]
+            near.append(dot(b_ref[leaf], jnp.concatenate(parts, axis=0)))
+        out = jnp.concatenate(near, axis=0) + dot(basis_ref[here, :], state)
         out_ref[here, :] = out.astype(BF)
         return carry
 
@@ -247,7 +290,41 @@
         cost_estimate=pl.CostEstimate(flops=600_000_000, bytes_accessed=5_000_000, transcendentals=0),
         name="own_up",
     )(points, g_own, low_up)
-    gathered = lax.all_gather(root_term, "leaf", axis=0, tiled=True)
+    near_blocks, root_term = lax.optimization_barrier((near_blocks, root_term))
+    other = lax.ppermute(root_term, "leaf", [(i, i ^ 1) for i in range(devices)])
+    near_cat = near_blocks.transpose(0, 2, 1, 3).reshape(leaf_dev, size, -1)
+    near_cat, other = lax.optimization_barrier((near_cat, other))
+    gathered = (root_term + other).astype(BF)
+    for bit in range(1, top_depth):
+        flip = 2**bit
+        if bit == 1:
+            local_coupling, gathered = lax.optimization_barrier((local_coupling, gathered))
+        if bit == 2:
+            g_late, gathered = lax.optimization_barrier((g_own, gathered))
+        other = lax.ppermute(gathered, "leaf", [(i, i ^ flip) for i in range(devices)])
+        if bit == 1:
+            s_cat = local_coupling[7:].transpose(0, 2, 1, 3).reshape(nodes, rank, -1)
+            s_cat, other = lax.optimization_barrier((s_cat, other))
+        if bit == 2:
+            e_groups, basis_groups = pl.pallas_call(
+                prep_kernel,
+                out_shape=(
+                    jax.ShapeDtypeStruct((nodes * rank, 4 * rank), BF),
+                    jax.ShapeDtypeStruct((leaf_dev * size, 4 * rank), BF),
+                ),
+                in_specs=[VMEM] * 2,
+                out_specs=(VMEM, VMEM),
+                compiler_params=PARAMS,
+                cost_estimate=pl.CostEstimate(flops=400_000_000, bytes_accessed=5_000_000, transcendentals=0),
+                name="prepare_down",
+            )(g_late, low_up)
+            e_groups, basis_groups, other = lax.optimization_barrier(
+                (e_groups, basis_groups, other)
+            )
+        upper = (own & flip) > 0
+        gathered = jnp.concatenate(
+            [jnp.where(upper, other, gathered), jnp.where(upper, gathered, other)], axis=0
+        )
 
     steps = jnp.arange(2, top_depth)
     ancestors = (devices + own) >> (top_depth - steps)
@@ -269,23 +346,6 @@
 
     first_leaf = (own - 1) * leaf_dev
     near_pos = jnp.where(near_lists >= 0, near_lists - first_leaf, 3 * leaf_dev).reshape(-1)
-    near_cat = near_blocks.transpose(0, 2, 1, 3).reshape(leaf_dev, size, -1)
-    near_rows = pl.pallas_call(
-        functools.partial(near_kernel, leaf_dev, size),
-        out_shape=jax.ShapeDtypeStruct((leaf_dev * size, vecs), F32),
-        in_specs=[SMEM, VMEM] + [pl.BlockSpec(memory_space=pl.ANY)] * 3,
-        out_specs=VMEM,
-        scratch_shapes=[
-            pltpu.VMEM(((3 * leaf_dev + 1) * size, vecs), BF),
-            pltpu.SemaphoreType.DMA((3,)),
-        ],
-        compiler_params=PARAMS,
-        cost_estimate=pl.CostEstimate(
-            flops=2_000_000_000, bytes_accessed=20_000_000, transcendentals=0
-        ),
-        name="near_field",
-    )(near_pos, near_cat, x_before, points, x_after)
-
     far_lists = local_lists[7:]
     row = jnp.arange(7, 2 * leaf_dev - 1)
     width = jnp.zeros_like(row)
@@ -293,35 +353,43 @@
         width = jnp.where(row >= 2**k - 1, 2**k, width)
     start = 3 * (width - 8) - (own - 1) * width
     far_pos = jnp.where(far_lists >= 0, far_lists + start[:, None], 3 * nodes).reshape(-1)
-    s_cat = local_coupling[7:].transpose(0, 2, 1, 3).reshape(nodes, rank, -1)
-    e_tiled = jnp.tile(local_transfer[7:], (1, 1, 4)).reshape(nodes * rank, 4 * rank)
-    basis_tiled = jnp.tile(leaf_basis, (1, 1, 4)).reshape(leaf_dev * size, 4 * rank)
+    any_space = pl.BlockSpec(memory_space=pl.ANY)
     return pl.pallas_call(
-        functools.partial(far_kernel, rank, leaf_dev),
+        functools.partial(field_kernel, rank, leaf_dev, size),
         out_shape=jax.ShapeDtypeStruct((leaf_dev * size, vecs), BF),
-        in_specs=[SMEM] + [VMEM] * 10,
+        in_specs=[SMEM] * 2 + [any_space] * 11,
         out_specs=VMEM,
         scratch_shapes=[
+            pltpu.VMEM(((3 * leaf_dev + 1) * size, vecs), BF),
+            pltpu.VMEM(g_own.shape, BF),
+            pltpu.VMEM(g_own.shape, BF),
+            pltpu.VMEM(near_cat.shape, BF),
+            pltpu.VMEM(s_cat.shape, BF),
+            pltpu.VMEM(e_groups.shape, BF),
+            pltpu.VMEM(basis_groups.shape, BF),
             pltpu.VMEM(((3 * nodes + 1) * rank, vecs), BF),
             pltpu.VMEM(((nodes + 4) * rank, vecs), BF),
+            pltpu.SemaphoreType.DMA((10 + depth - 2,)),
         ],
         compiler_params=PARAMS,
         cost_estimate=pl.CostEstimate(
-            flops=2_000_000_000, bytes_accessed=20_000_000, transcendentals=0
+            flops=4_000_000_000, bytes_accessed=30_000_000, transcendentals=0
         ),
-        name="far_field",
+        name="near_and_far",
     )(
+        near_pos,
         far_pos,
         x_before,
+        points,
         x_after,
         g_before,
         g_after,
+        near_cat,
+        s_cat,
+        e_groups,
+        basis_groups,
         coeff_own,
-        s_cat,
-        e_tiled,
-        basis_tiled,
         down_two,
-        near_rows,
     )
 
 

time: 210 us -> 162 us (0.77)
  blocking collectives: 47.6 us -> 0 us
  local copies, waits for them, and re-layouts: 87.7 us -> 55.3 us
  waiting for transfers between devices: 0.01 us -> 28.1 us
  starting transfers between devices: 11.3 us -> 26 us
  Pallas kernels: 58.5 us -> 47 us
    all_gather x1 -> x0, blocking collectives: 47.6 us -> none  [shards(): gathered = lax.all_gather(root_term, 'leaf', axis=0, tiled=True)]
    ppermute x0 -> x5, waiting for transfers between devices: none -> 28.1 us  [the longest x4 28.1 us: shards(): lax.ppermute(gathered, 'leaf', [(i, i ^ flip) for i in range(devices)])]
    another operation x6 -> x0, local copies, waits for them, and re-layouts: 26.4 us -> none  [the longest x3 15.3 us: shards(): jnp.tile(local_transfer[7:], (1, 1, 4)).reshape(nodes * rank, 4 * rank)]
    optimization_barrier x0 -> x3, local copies, waits for them, and re-layouts: none -> 24.3 us  [the longest x1 8.99 us: shards(): near_cat, other = lax.optimization_barrier((near_cat, other))]
    reshape x2 -> x0, local copies, waits for them, and re-layouts: 16.7 us -> none  [the longest x1 9.05 us: shards(): near_cat = near_blocks.transpose(0, 2, 1, 3).reshape(leaf_dev, size, -1)]
    ppermute x0 -> x5, starting transfers between devices: none -> 13.8 us  [the longest x4 13.4 us: shards(): lax.ppermute(gathered, 'leaf', [(i, i ^ flip) for i in range(devices)])]
    pallas_call x2, Pallas kernels: 46.2 us -> 34.7 us  [the longest x1 28.7 us: shards(): pl.pallas_call(functools.partial(field_kernel, rank, leaf_dev, size), out...]
    unnamed x30 -> x24, local copies, waits for them, and re-layouts: 15.3 us -> 7.78 us
  transfers between devices with their start and end apart: 4 -> 9, of which waited for: 0 -> 2; matrix products, arithmetic and copies ran while one was open for 44% -> 26% of each run, Pallas kernels for 13% -> 11%
where the time goes in v2:
time: 162 us; the launch traced here: 161 us
  local copies, waits for them, and re-layouts  55.3 us (34%)
  Pallas kernels  47 us (29%)
  waiting for transfers between devices  28.1 us (17%)
  starting transfers between devices  26 us (16%)
  other arithmetic  4.1 us (3%)
    pallas_call x1, Pallas kernels, shards(): pl.pallas_call(functools.partial(field_kernel, rank, leaf_dev, size), out...  28.7 us
    ppermute x4, waiting for transfers between devices, shards(): lax.ppermute(gathered, 'leaf', [(i, i ^ flip) for i in range(devices)])  28.1 us
    ppermute x4, starting transfers between devices, shards(): lax.ppermute(gathered, 'leaf', [(i, i ^ flip) for i in range(devices)])  13.4 us
    pallas_call x1, Pallas kernels, shards(): pl.pallas_call(functools.partial(own_kernel, rank, leaf_dev), out_shape=(...  9.64 us
    optimization_barrier x1, local copies, waits for them, and re-layouts, shards(): near_cat, other = lax.optimization_barrier((near_cat, other))  8.99 us
    unnamed x24, local copies, waits for them, and re-layouts  7.78 us
    optimization_barrier x1, local copies, waits for them, and re-layouts, shards(): near_blocks, root_term = lax.optimization_barrier((near_blocks, root_term))  7.77 us
    optimization_barrier x1, local copies, waits for them, and re-layouts, shards(): s_cat, other = lax.optimization_barrier((s_cat, other))  7.58 us
  transfers between devices with their start and end apart: 9, of which 2 were waited for; matrix products, arithmetic and copies ran while one was open for 26% of the time, Pallas kernels for 11%

profile of v2, /device:TPU:0, one launch (start us, length us, event | category | flops | bytes accessed | tf_op | source)
XLA Modules:
  0.0 160.9 jit_solution(10611027624113748781)
XLA Ops:
  0.0 2.3 %slice.28 = bf16[240,32,32]{0,2,1:T(8,128)(2,1)} slice(bf16[255,32,32]{0,2,1:T(8,128)(2,1)} %param.12), slice={[15:255], [0:32], [0:32]} | slice | bytes 983040 | tf_op jit(solution)/shard_map/slice | solution.py:269
  2.3 3.7 %copy.25 = bf16[128,64,32]{1,2,0:T(8,128)(2,1)} copy(bf16[128,64,32]{0,2,1:T(8,128)(2,1)} %param.11) | data formatting | bytes 1048576 | tf_op args[1]
  5.9 1.8 %copy.26 = bf16[32,32,4,64]{3,2,1,0:T(4,128)(2,1)S(1)} copy(bf16[32,32,4,64]{3,1,2,0:T(8,128)(2,1)} %bitcast.42) | data formatting | bytes 1048576 | tf_op jit(solution)/shard_map/transpose | solution.py:266
  7.7 1.5 reshape.92
  9.2 3.6 %copy.42 = bf16[240,32,32]{2,1,0:T(8,128)(2,1)} copy(bf16[240,32,32]{0,2,1:T(8,128)(2,1)} %slice.28) | data formatting | bytes 983040
  12.8 2.6 %copy.41 = bf16[30,32,256]{2,1,0:T(8,128)(2,1)} copy(bf16[30,32,256]{1,2,0:T(8,128)(2,1)} %bitcast.41) | data formatting | bytes 983040 | tf_op jit(solution)/shard_map/reshape | solution.py:238
  15.4 2.1 %pad_maximum_fusion.g_ref = bf16[62,32,256]{2,1,0:T(8,128)(2,1)} fusion(bf16[30,32,256]{2,1,0:T(8,128)(2,1)} %copy.41, bf16[32,32,256]{2,1,0:T(8,128)(2,1)S(1)} %copy-done.3), kind=kLoop, calls=%fused_computation.4 | loop fusion | flops 507904 | bytes 2031616 | tf_op jit(solution)/shard_map/concatenate | solution.py:269
  17.5 1.4 collective-permute-start.3
  18.9 4.0 %collective-permute-start.2 = (bf16[62,32,256]{2,1,0:T(8,128)(2,1)}, bf16[62,32,256]{2,1,0:T(8,128)(2,1)}, u32[]{:S(2)}, u32[]{:S(2)}) collective-permute-start(bf16[62,32,256]{2,1,0:T(8,128)(2,1)} %pad_maximum_fusion.g_ref), channel_id=1, source_target_pairs={{0,1},{1,2},{2,3},{3,4},{4,5},{5,6},{6,7},{7,8},{8,9},{9,10},{10,1... | collective-permute-start | bytes 3047432 | tf_op jit(solution)/shard_map/ppermute | solution.py:270
  22.9 1.3 collective-permute-start.1
  24.2 5.5 %collective-permute-start = (bf16[8192,128]{1,0:T(8,128)(2,1)}, bf16[8192,128]{1,0:T(8,128)(2,1)}, u32[]{:S(2)}, u32[]{:S(2)}) collective-permute-start(bf16[8192,128]{1,0:T(8,128)(2,1)} %xo_hbm.1), channel_id=1, source_target_pairs={{0,1},{1,2},{2,3},{3,4},{4,5},{5,6},{6,7},{7,8},{8,9},{9,10},{10,1... | collective-permute-start | bytes 6291464 | tf_op jit(solution)/shard_map/ppermute | solution.py:262
  29.7 0.1 slice_bitcast_fusion.2
  29.9 0.1 slice_bitcast_fusion.1
  30.0 0.9 fusion.1
  30.9 0.4 copy.30
  31.3 0.1 reshape.95
  31.4 0.4 copy.31
  31.8 0.1 reshape.96
  31.9 0.4 copy.43
  32.3 1.2 copy.29
  33.5 0.1 stack.15
  33.6 0.6 pad_maximum_fusion.2.low_ref
  34.3 9.6 %own_up.1 = (bf16[7936,128]{1,0:T(8,128)(2,1)}, f32[32,128]{1,0:T(8,128)}) custom-call(bf16[8192,128]{1,0:T(8,128)(2,1)} %xo_hbm.1, bf16[62,32,256]{2,1,0:T(8,128)(2,1)} %pad_maximum_fusion.g_ref, bf16[4,32,256]{2,1,0:T(8,128)(2,1)} %pad_maximum_fusion.2.low_ref), custom_call_target="tpu_custom_call" | custom-call | flops 600000000 | bytes 5000000 | tf_op jit(solution)/shard_map/own_up/pallas_call | solution.py:281
  43.9 0.4 collective-permute-start.4
  44.3 0.1 add_select_fusion
  44.4 0.0 copy-start.2
  44.4 7.8 %copy.33 = bf16[128,6,64,64]{0,3,1,2:T(8,128)(2,1)} copy(bf16[128,6,64,64]{0,3,2,1:T(8,128)(2,1)} %param.18) | data formatting | bytes 12582912 | tf_op jit(solution)/shard_map/optimization_barrier | solution.py:293
  52.2 0.0 collective-permute-done.4
  52.2 3.3 %collective-permute-start.5 = (bf16[32,128]{1,0:T(8,128)(2,1)S(1)}, bf16[32,128]{1,0:T(8,128)(2,1)S(1)}, u32[]{:S(2)}, u32[]{:S(2)}) collective-permute-start(bf16[32,128]{1,0:T(8,128)(2,1)S(1)} %add_convert_fusion), channel_id=1, source_target_pairs={{0,2},{1,3},{2,0},{3,1},{4,6},{5,7},{6,4},{7,5},{8,10},{9,11},{10,... | collective-permute-start | bytes 24584 | tf_op jit(solution)/shard_map/ppermute | solution.py:304
  55.5 2.4 %slice_bitcast_fusion = bf16[248,32,8,32]{0,3,1,2:T(8,128)(2,1)S(1)} fusion(bf16[255,8,32,32]{0,3,2,1:T(8,128)(2,1)S(1)} %copy-done.2), kind=kLoop, calls=%fused_computation.3 | loop fusion | bytes 8126464 | tf_op jit(solution)/shard_map/transpose | solution.py:306
  58.0 0.0 copy-start.8
  58.0 0.0 copy-start.5
  58.0 2.4 %copy.34 = bf16[248,32,8,32]{0,3,2,1:T(8,128)(2,1)} copy(bf16[248,32,8,32]{0,3,1,2:T(8,128)(2,1)S(1)} %slice_bitcast_fusion) | data formatting | bytes 8126464 | tf_op jit(solution)/shard_map/transpose | solution.py:306
  60.4 26.9 %collective-permute-done.5 = bf16[32,128]{1,0:T(8,128)(2,1)S(1)} collective-permute-done((bf16[32,128]{1,0:T(8,128)(2,1)S(1)}, bf16[32,128]{1,0:T(8,128)(2,1)S(1)}, u32[]{:S(2)}, u32[]{:S(2)}) %collective-permute-start.5) | collective-permute-done | bytes 8224 | tf_op jit(solution)/shard_map/ppermute | solution.py:304
  87.3 2.2 %collective-permute-start.6 = (bf16[64,128]{1,0:T(8,128)(2,1)S(1)}, bf16[64,128]{1,0:T(8,128)(2,1)S(1)}, u32[]{:S(2)}, u32[]{:S(2)}) collective-permute-start(bf16[64,128]{1,0:T(8,128)(2,1)S(1)} %pad_maximum_fusion.5), channel_id=1, source_target_pairs={{0,4},{1,5},{2,6},{3,7},{4,0},{5,1},{6,2},{7,3},{8,12},{9,13},{10,... | collective-permute-start | bytes 49160 | tf_op jit(solution)/shard_map/ppermute | solution.py:304
  89.6 6.0 %prepare_down.1 = (bf16[7936,128]{1,0:T(8,128)(2,1)}, bf16[8192,128]{1,0:T(8,128)(2,1)}) custom-call(bf16[62,32,256]{2,1,0:T(8,128)(2,1)} %pad_maximum_fusion.g_ref, bf16[4,32,256]{2,1,0:T(8,128)(2,1)} %pad_maximum_fusion.2.low_ref), custom_call_target="tpu_custom_call" | custom-call | flops 400000000 | bytes 5000000 | tf_op jit(solution)/shard_map/prepare_down/pallas_call | solution.py:309
  95.6 0.0 collective-permute-done.6
  95.6 4.8 %collective-permute-start.7 = (bf16[128,128]{1,0:T(8,128)(2,1)S(1)}, bf16[128,128]{1,0:T(8,128)(2,1)S(1)}, u32[]{:S(2)}, u32[]{:S(2)}) collective-permute-start(bf16[128,128]{1,0:T(8,128)(2,1)S(1)} %pad_maximum_fusion.4), channel_id=1, source_target_pairs={{0,8},{1,9},{2,10},{3,11},{4,12},{5,13},{6,14},{7,15},{8,0},{9,1},... | collective-permute-start | bytes 98312 | tf_op jit(solution)/shard_map/ppermute | solution.py:304
  100.4 0.1 copy.35
  100.5 0.6 gather_fusion
  101.0 0.1 gather.12
  101.1 1.2 collective-permute-done.7
  102.3 3.1 %collective-permute-start.8 = (bf16[256,128]{1,0:T(8,128)(2,1)S(1)}, bf16[256,128]{1,0:T(8,128)(2,1)S(1)}, u32[]{:S(2)}, u32[]{:S(2)}) collective-permute-start(bf16[256,128]{1,0:T(8,128)(2,1)S(1)} %pad_maximum_fusion.3), channel_id=1, source_target_pairs={{0,16},{1,17},{2,18},{3,19},{4,20},{5,21},{6,22},{7,23},{8,24},{9,... | collective-permute-start | bytes 196616 | tf_op jit(solution)/shard_map/ppermute | solution.py:304
  105.4 0.5 compare_select_fusion.pos_ref
  106.0 1.2 gather_fusion.2
  107.1 0.1 copy.23
  107.2 0.7 reshape.89.near_pos
  108.0 0.1 copy.24
  108.1 0.7 reshape.90.far_pos
  108.8 0.6 gather_fusion.1
  109.4 0.1 copy.37
  109.5 0.8 reshape.102.s_ref
  110.3 0.2 copy.36
  110.5 0.8 reshape.101.up_ref
  111.3 0.8 copy.38
  112.1 9.0 %copy.39.b_hbm = bf16[128,64,384]{2,1,0:T(8,128)(2,1)} copy(bf16[128,64,384]{0,2,1:T(8,128)(2,1)} %bitcast.39) | data formatting | bytes 12582912 | tf_op jit(solution)/shard_map/optimization_barrier | solution.py:296
  121.1 7.6 %copy.40.s_hbm = bf16[248,32,256]{2,1,0:T(8,128)(2,1)} copy(bf16[248,32,256]{0,2,1:T(8,128)(2,1)} %bitcast.40) | data formatting | bytes 8126464 | tf_op jit(solution)/shard_map/optimization_barrier | solution.py:307
  128.7 0.0 collective-permute-done.8
  128.7 0.7 pad_maximum_fusion.1.g_ref
  129.4 2.7 %top_tree.1.down_hbm = bf16[128,128]{1,0:T(8,128)(2,1)} custom-call(s32[24]{0:T(128)} %compare_select_fusion.pos_ref, bf16[512,128]{1,0:T(8,128)(2,1)} %pad_maximum_fusion.1.g_ref, bf16[3,32,256]{2,1,0:T(8,128)(2,1)} %reshape.101.up_ref, bf16[3,32,256]{2,1,0:T(8,128)(2,1)} %reshape.102.s_ref, bf16[3,32,32]{2,1,0:T(8,128)(2,1)} %gather_fusion.2, ...), custom_call_target="tpu_custom_call" | custom-call | flops 50000000 | bytes 1000000 | tf_op jit(solution)/shard_map/top_tree/pallas_call | solution.py:336
  132.1 0.0 collective-permute-done.3.ga_hbm
  132.1 0.0 collective-permute-done.2.gb_hbm
  132.1 0.0 collective-permute-done.1.xa_hbm
  132.1 28.7 %near_and_far.1 = bf16[8192,128]{1,0:T(8,128)(2,1)} custom-call(s32[768]{0:T(1024)} %reshape.89.near_pos, s32[1984]{0:T(1024)} %reshape.90.far_pos, bf16[8192,128]{1,0:T(8,128)(2,1)} %collective-permute-done.xb_hbm, bf16[8192,128]{1,0:T(8,128)(2,1)} %xo_hbm.1, bf16[8192,128]{1,0:T(8,128)(2,1)} %collective-permute-done.1.xa_hbm, ...), custom_call_target="tpu_custom_call" | custom-call | flops 4000000000 | bytes 30000000 | tf_op jit(solution)/shard_map/near_and_far/pallas_call | solution.py:357
  (36 shorter events, 0.2 us)
Async XLA Ops:
  0.0 108.8 %copy-start = (bf16[32,8,32,32]{3,2,1,0:T(8,128)(2,1)S(1)}, bf16[32,8,32,32]{3,2,1,0:T(8,128)(2,1)}, u32[]{:S(2)}) copy-start(bf16[32,8,32,32]{3,2,1,0:T(8,128)(2,1)} %param.16) | copy-start | bytes 1572868
  9.2 6.2 %copy-start.3 = (bf16[32,32,256]{2,1,0:T(8,128)(2,1)S(1)}, bf16[32,32,256]{2,1,0:T(8,128)(2,1)}, u32[]{:S(2)}) copy-start(bf16[32,32,256]{2,1,0:T(8,128)(2,1)} %reshape.92) | copy-start | bytes 1572868
  12.8 16.9 %copy-start.1 = (bf16[255,32,32]{0,2,1:T(8,128)(2,1)S(1)}, bf16[255,32,32]{0,2,1:T(8,128)(2,1)}, u32[]{:S(2)}) copy-start(bf16[255,32,32]{0,2,1:T(8,128)(2,1)} %param.12) | copy-start | bytes 1566724
  17.5 14.4 %slice-start = ((bf16[255,32,32]{0,2,1:T(8,128)(2,1)}), bf16[1,32,32]{0,2,1:T(8,128)(2,1)S(1)}, s32[]{:S(2)}) async-start(bf16[255,32,32]{0,2,1:T(8,128)(2,1)} %param.12), calls=%async_computation | async-start | bytes 524288 | tf_op jit(solution)/shard_map/slice | solution.py:278
  17.5 114.6 %collective-permute-start.3 = (bf16[62,32,256]{2,1,0:T(8,128)(2,1)}, bf16[62,32,256]{2,1,0:T(8,128)(2,1)}, u32[]{:S(2)}, u32[]{:S(2)}) collective-permute-start(bf16[62,32,256]{2,1,0:T(8,128)(2,1)} %pad_maximum_fusion.g_ref), channel_id=1, source_target_pairs={{1,0},{2,1},{3,2},{4,3},{5,4},{6,5},{7,6},{8,7},{9,8},{10,9},{11,1... | collective-permute-start | bytes 3047432 | tf_op jit(solution)/shard_map/ppermute | solution.py:271
  18.9 113.2 %collective-permute-start.2 = (bf16[62,32,256]{2,1,0:T(8,128)(2,1)}, bf16[62,32,256]{2,1,0:T(8,128)(2,1)}, u32[]{:S(2)}, u32[]{:S(2)}) collective-permute-start(bf16[62,32,256]{2,1,0:T(8,128)(2,1)} %pad_maximum_fusion.g_ref), channel_id=1, source_target_pairs={{0,1},{1,2},{2,3},{3,4},{4,5},{5,6},{6,7},{7,8},{8,9},{9,10},{10,1... | collective-permute-start | bytes 3047432 | tf_op jit(solution)/shard_map/ppermute | solution.py:270
  22.9 109.2 %collective-permute-start.1 = (bf16[8192,128]{1,0:T(8,128)(2,1)}, bf16[8192,128]{1,0:T(8,128)(2,1)}, u32[]{:S(2)}, u32[]{:S(2)}) collective-permute-start(bf16[8192,128]{1,0:T(8,128)(2,1)} %xo_hbm.1), channel_id=1, source_target_pairs={{1,0},{2,1},{3,2},{4,3},{5,4},{6,5},{7,6},{8,7},{9,8},{10,9},{11,1... | collective-permute-start | bytes 6291464 | tf_op jit(solution)/shard_map/ppermute | solution.py:263
  24.2 107.9 %collective-permute-start = (bf16[8192,128]{1,0:T(8,128)(2,1)}, bf16[8192,128]{1,0:T(8,128)(2,1)}, u32[]{:S(2)}, u32[]{:S(2)}) collective-permute-start(bf16[8192,128]{1,0:T(8,128)(2,1)} %xo_hbm.1), channel_id=1, source_target_pairs={{0,1},{1,2},{2,3},{3,4},{4,5},{5,6},{6,7},{7,8},{8,9},{9,10},{10,1... | collective-permute-start | bytes 6291464 | tf_op jit(solution)/shard_map/ppermute | solution.py:262
  31.8 12.5 %copy-start.9 = (s32[128,6]{0,1:T(8,128)S(1)}, s32[128,6]{0,1:T(8,128)}, u32[]{:S(2)}) copy-start(s32[128,6]{0,1:T(8,128)} %param.19) | copy-start | bytes 9220
  31.8 12.5 %copy-start.7 = (s32[255,8]{0,1:T(8,128)S(1)}, s32[255,8]{0,1:T(8,128)}, u32[]{:S(2)}) copy-start(s32[255,8]{0,1:T(8,128)} %param.15) | copy-start | bytes 24484
  43.9 8.3 %collective-permute-start.4 = (f32[32,128]{1,0:T(8,128)}, f32[32,128]{1,0:T(8,128)S(1)}, u32[]{:S(2)}, u32[]{:S(2)}) collective-permute-start(f32[32,128]{1,0:T(8,128)} %get-tuple-element.24), channel_id=1, source_target_pairs={{0,1},{1,0},{2,3},{3,2},{4,5},{5,4},{6,7},{7,6},{8,9},{9,8},{10,11... | collective-permute-start | bytes 49160 | tf_op jit(solution)/shard_map/ppermute | solution.py:294
  44.4 7.8 %copy-start.6 = (f32[32,128]{1,0:T(8,128)S(1)}, f32[32,128]{1,0:T(8,128)}, u32[]{:S(2)}) copy-start(f32[32,128]{1,0:T(8,128)} %get-tuple-element.24) | copy-start | bytes 49156
  44.4 11.1 %copy-start.2 = (bf16[255,8,32,32]{0,3,2,1:T(8,128)(2,1)S(1)}, bf16[255,8,32,32]{0,3,2,1:T(8,128)(2,1)}, u32[]{:S(2)}) copy-start(bf16[255,8,32,32]{0,3,2,1:T(8,128)(2,1)} %param.14) | copy-start | bytes 12533764
  52.2 35.1 %collective-permute-start.5 = (bf16[32,128]{1,0:T(8,128)(2,1)S(1)}, bf16[32,128]{1,0:T(8,128)(2,1)S(1)}, u32[]{:S(2)}, u32[]{:S(2)}) collective-permute-start(bf16[32,128]{1,0:T(8,128)(2,1)S(1)} %add_convert_fusion), channel_id=1, source_target_pairs={{0,2},{1,3},{2,0},{3,1},{4,6},{5,7},{6,4},{7,5},{8,10},{9,11},{10,... | collective-permute-start | bytes 24584 | tf_op jit(solution)/shard_map/ppermute | solution.py:304
  58.0 42.4 %copy-start.8 = (s32[32,8]{0,1:T(8,128)S(1)}, s32[32,8]{0,1:T(8,128)}, u32[]{:S(2)}) copy-start(s32[32,8]{0,1:T(8,128)} %param.17) | copy-start | bytes 3076
  58.0 48.0 %copy-start.5 = (bf16[32,32,32]{2,1,0:T(8,128)(2,1)S(1)}, bf16[32,32,32]{2,1,0:T(8,128)(2,1)}, u32[]{:S(2)}) copy-start(bf16[32,32,32]{2,1,0:T(8,128)(2,1)} %param.13) | copy-start | bytes 196612
  60.4 49.9 %slice-start.1 = ((bf16[32,32,32]{2,1,0:T(8,128)(2,1)}), bf16[24,32,32]{2,1,0:T(8,128)(2,1)S(1)}, s32[]{:S(2)}) async-start(bf16[32,32,32]{2,1,0:T(8,128)(2,1)} %param.13), calls=%async_computation.1 | async-start | bytes 393216 | tf_op jit(solution)/shard_map/slice | solution.py:345
  87.3 23.9 %copy-start.4 = (bf16[8,32,32]{0,2,1:T(8,128)(2,1)S(1)}, bf16[8,32,32]{0,2,1:T(8,128)(2,1)}, u32[]{:S(2)}) copy-start(bf16[8,32,32]{0,2,1:T(8,128)(2,1)} %get-tuple-element.39) | copy-start | bytes 49156
  87.3 8.3 %collective-permute-start.6 = (bf16[64,128]{1,0:T(8,128)(2,1)S(1)}, bf16[64,128]{1,0:T(8,128)(2,1)S(1)}, u32[]{:S(2)}, u32[]{:S(2)}) collective-permute-start(bf16[64,128]{1,0:T(8,128)(2,1)S(1)} %pad_maximum_fusion.5), channel_id=1, source_target_pairs={{0,4},{1,5},{2,6},{3,7},{4,0},{5,1},{6,2},{7,3},{8,12},{9,13},{10,... | collective-permute-start | bytes 49160 | tf_op jit(solution)/shard_map/ppermute | solution.py:304
  95.6 6.7 %collective-permute-start.7 = (bf16[128,128]{1,0:T(8,128)(2,1)S(1)}, bf16[128,128]{1,0:T(8,128)(2,1)S(1)}, u32[]{:S(2)}, u32[]{:S(2)}) collective-permute-start(bf16[128,128]{1,0:T(8,128)(2,1)S(1)} %pad_maximum_fusion.4), channel_id=1, source_target_pairs={{0,8},{1,9},{2,10},{3,11},{4,12},{5,13},{6,14},{7,15},{8,0},{9,1},... | collective-permute-start | bytes 98312 | tf_op jit(solution)/shard_map/ppermute | solution.py:304
  102.3 26.3 %collective-permute-start.8 = (bf16[256,128]{1,0:T(8,128)(2,1)S(1)}, bf16[256,128]{1,0:T(8,128)(2,1)S(1)}, u32[]{:S(2)}, u32[]{:S(2)}) collective-permute-start(bf16[256,128]{1,0:T(8,128)(2,1)S(1)} %pad_maximum_fusion.3), channel_id=1, source_target_pairs={{0,16},{1,17},{2,18},{3,19},{4,20},{5,21},{6,22},{7,23},{8,24},{9,... | collective-permute-start | bytes 196616 | tf_op jit(solution)/shard_map/ppermute | solution.py:304

commit v3 on v2

--- a/solution.py
+++ b/solution.py
@@ -3,6 +3,7 @@
 import jax
 import jax.numpy as jnp
 from jax import lax
+from jax.experimental.layout import Layout, with_layout_constraint
 from jax.experimental import pallas as pl
 from jax.experimental.pallas import tpu as pltpu
 from jax.sharding import PartitionSpec as P
@@ -290,21 +291,23 @@
         cost_estimate=pl.CostEstimate(flops=600_000_000, bytes_accessed=5_000_000, transcendentals=0),
         name="own_up",
     )(points, g_own, low_up)
-    near_blocks, root_term = lax.optimization_barrier((near_blocks, root_term))
     other = lax.ppermute(root_term, "leaf", [(i, i ^ 1) for i in range(devices)])
-    near_cat = near_blocks.transpose(0, 2, 1, 3).reshape(leaf_dev, size, -1)
-    near_cat, other = lax.optimization_barrier((near_cat, other))
     gathered = (root_term + other).astype(BF)
     for bit in range(1, top_depth):
         flip = 2**bit
         if bit == 1:
-            local_coupling, gathered = lax.optimization_barrier((local_coupling, gathered))
+            near_blocks, local_coupling, gathered = lax.optimization_barrier(
+                (near_blocks, local_coupling, gathered)
+            )
         if bit == 2:
             g_late, gathered = lax.optimization_barrier((g_own, gathered))
         other = lax.ppermute(gathered, "leaf", [(i, i ^ flip) for i in range(devices)])
         if bit == 1:
+            near_cat = near_blocks.transpose(0, 2, 1, 3).reshape(leaf_dev, size, -1)
+            near_cat = with_layout_constraint(near_cat, Layout((0, 1, 2)))
             s_cat = local_coupling[7:].transpose(0, 2, 1, 3).reshape(nodes, rank, -1)
-            s_cat, other = lax.optimization_barrier((s_cat, other))
+            s_cat = with_layout_constraint(s_cat, Layout((0, 1, 2)))
+            near_cat, s_cat, other = lax.optimization_barrier((near_cat, s_cat, other))
         if bit == 2:
             e_groups, basis_groups = pl.pallas_call(
                 prep_kernel,

time: 162 us -> 144 us (0.89)
  waiting for transfers between devices: 28.1 us -> 10.7 us
  starting transfers between devices: 26 us -> 20.5 us
  local copies, waits for them, and re-layouts: 55.3 us -> 59.4 us
    ppermute x4, waiting for transfers between devices: 28.1 us -> 9.72 us  [shards(): lax.ppermute(gathered, 'leaf', [(i, i ^ flip) for i in range(devices)])]
    optimization_barrier x3 -> x1, local copies, waits for them, and re-layouts: 24.3 us -> 7.61 us  [shards(): lax.optimization_barrier((near_blocks, local_coupling, gathered))]
    reshape x0 -> x2, local copies, waits for them, and re-layouts: none -> 16.6 us  [the longest x1 9 us: shards(): near_cat = near_blocks.transpose(0, 2, 1, 3).reshape(leaf_dev, size, -1)]
    transpose x2, local copies, waits for them, and re-layouts: 4.82 us -> 11.5 us  [shards(): s_cat = local_coupling[7:].transpose(0, 2, 1, 3).reshape(nodes, rank, -1)]
    ppermute x4, starting transfers between devices: 13.4 us -> 7.85 us  [shards(): lax.ppermute(gathered, 'leaf', [(i, i ^ flip) for i in range(devices)])]
    unnamed x24 -> x18, local copies, waits for them, and re-layouts: 7.78 us -> 5.93 us
  transfers between devices with their start and end apart: 9 -> 9, of which waited for: 2 -> 3; matrix products, arithmetic and copies ran while one was open for 26% -> 34% of each run, Pallas kernels for 11% -> 13%
where the time goes in v3:
time: 144 us; the launch traced here: 143 us
  local copies, waits for them, and re-layouts  59.4 us (41%)
  Pallas kernels  46.9 us (33%)
  starting transfers between devices  20.5 us (14%)
  waiting for transfers between devices  10.7 us (7%)
  other arithmetic  4.85 us (3%)
    pallas_call x1, Pallas kernels, shards(): pl.pallas_call(functools.partial(field_kernel, rank, leaf_dev, size), out...  28.7 us
    transpose x2, local copies, waits for them, and re-layouts, shards(): s_cat = local_coupling[7:].transpose(0, 2, 1, 3).reshape(nodes, rank, -1)  11.5 us
    ppermute x4, waiting for transfers between devices, shards(): lax.ppermute(gathered, 'leaf', [(i, i ^ flip) for i in range(devices)])  9.72 us
    pallas_call x1, Pallas kernels, shards(): pl.pallas_call(functools.partial(own_kernel, rank, leaf_dev), out_shape=(...  9.59 us
    reshape x1, local copies, waits for them, and re-layouts, shards(): near_cat = near_blocks.transpose(0, 2, 1, 3).reshape(leaf_dev, size, -1)  9 us
    ppermute x4, starting transfers between devices, shards(): lax.ppermute(gathered, 'leaf', [(i, i ^ flip) for i in range(devices)])  7.85 us
    optimization_barrier x1, local copies, waits for them, and re-layouts, shards(): lax.optimization_barrier((near_blocks, local_coupling, gathered))  7.61 us
    reshape x1, local copies, waits for them, and re-layouts, shards(): s_cat = local_coupling[7:].transpose(0, 2, 1, 3).reshape(nodes, rank, -1)  7.57 us
  transfers between devices with their start and end apart: 9, of which 3 were waited for; matrix products, arithmetic and copies ran while one was open for 34% of the time, Pallas kernels for 13%

profile of v3, /device:TPU:0, one launch (start us, length us, event | category | flops | bytes accessed | tf_op | source)
XLA Modules:
  0.0 142.7 jit_solution(16844254124990488537)
XLA Ops:
  0.0 1.4 %slice.28 = bf16[240,32,32]{0,2,1:T(8,128)(2,1)S(1)} slice(bf16[255,32,32]{0,2,1:T(8,128)(2,1)} %param.12), slice={[15:255], [0:32], [0:32]} | slice | bytes 983040 | tf_op jit(solution)/shard_map/slice | solution.py:270
  1.5 2.6 %copy.42 = bf16[240,32,32]{2,1,0:T(8,128)(2,1)} copy(bf16[240,32,32]{0,2,1:T(8,128)(2,1)S(1)} %slice.28) | data formatting | bytes 983040
  4.1 2.5 %copy.41 = bf16[30,32,256]{2,1,0:T(8,128)(2,1)} copy(bf16[30,32,256]{1,2,0:T(8,128)(2,1)} %bitcast.41) | data formatting | bytes 983040 | tf_op jit(solution)/shard_map/reshape | solution.py:239
  6.6 2.8 %copy.25 = bf16[128,64,32]{1,2,0:T(8,128)(2,1)S(1)} copy(bf16[128,64,32]{0,2,1:T(8,128)(2,1)} %param.11) | data formatting | bytes 1048576 | tf_op args[1]
  9.4 1.5 %copy.26 = bf16[32,32,4,64]{3,2,1,0:T(4,128)(2,1)} copy(bf16[32,32,4,64]{3,1,2,0:T(8,128)(2,1)S(1)} %bitcast.42) | data formatting | bytes 1048576 | tf_op jit(solution)/shard_map/transpose | solution.py:267
  10.9 2.1 %reshape.92 = bf16[32,32,256]{2,1,0:T(8,128)(2,1)S(1)} reshape(bf16[32,32,4,64]{3,2,1,0:T(4,128)(2,1)} %copy.26) | data formatting | bytes 1048576 | tf_op jit(solution)/shard_map/reshape | solution.py:268
  13.1 2.1 %pad_maximum_fusion.g_ref = bf16[62,32,256]{2,1,0:T(8,128)(2,1)} fusion(bf16[30,32,256]{2,1,0:T(8,128)(2,1)} %copy.41, bf16[32,32,256]{2,1,0:T(8,128)(2,1)S(1)} %reshape.92), kind=kLoop, calls=%fused_computation.4 | loop fusion | flops 507904 | bytes 2031616 | tf_op jit(solution)/shard_map/concatenate | solution.py:270
  15.2 3.5 %collective-permute-start.2 = (bf16[62,32,256]{2,1,0:T(8,128)(2,1)}, bf16[62,32,256]{2,1,0:T(8,128)(2,1)}, u32[]{:S(2)}, u32[]{:S(2)}) collective-permute-start(bf16[62,32,256]{2,1,0:T(8,128)(2,1)} %pad_maximum_fusion.g_ref), channel_id=1, source_target_pairs={{0,1},{1,2},{2,3},{3,4},{4,5},{5,6},{6,7},{7,8},{8,9},{9,10},{10,1... | collective-permute-start | bytes 3047432 | tf_op jit(solution)/shard_map/ppermute | solution.py:271
  18.6 1.3 collective-permute-start.3
  19.9 5.5 %collective-permute-start = (bf16[8192,128]{1,0:T(8,128)(2,1)}, bf16[8192,128]{1,0:T(8,128)(2,1)}, u32[]{:S(2)}, u32[]{:S(2)}) collective-permute-start(bf16[8192,128]{1,0:T(8,128)(2,1)} %xo_hbm.1), channel_id=1, source_target_pairs={{0,1},{1,2},{2,3},{3,4},{4,5},{5,6},{6,7},{7,8},{8,9},{9,10},{10,1... | collective-permute-start | bytes 6291464 | tf_op jit(solution)/shard_map/ppermute | solution.py:263
  25.4 1.3 collective-permute-start.1
  26.7 0.9 fusion.1
  27.7 0.1 slice_bitcast_fusion.1
  27.8 0.1 slice_bitcast_fusion.2
  27.9 1.2 copy.29
  29.2 0.1 stack.15
  29.3 0.0 copy-start.4
  29.3 0.0 copy-start.6
  29.3 0.4 copy.31
  29.7 0.1 reshape.96
  29.8 0.4 copy.43
  30.2 0.4 copy.30
  30.6 0.1 reshape.95
  30.7 0.6 pad_maximum_fusion.2.low_ref
  31.3 9.6 %own_up.1 = (bf16[7936,128]{1,0:T(8,128)(2,1)}, f32[32,128]{1,0:T(8,128)}) custom-call(bf16[8192,128]{1,0:T(8,128)(2,1)} %xo_hbm.1, bf16[62,32,256]{2,1,0:T(8,128)(2,1)} %pad_maximum_fusion.g_ref, bf16[4,32,256]{2,1,0:T(8,128)(2,1)} %pad_maximum_fusion.2.low_ref), custom_call_target="tpu_custom_call" | custom-call | flops 600000000 | bytes 5000000 | tf_op jit(solution)/shard_map/own_up/pallas_call | solution.py:282
  40.9 1.1 collective-permute-start.4
  42.1 0.1 add_select_fusion
  42.2 0.9 collective-permute-done.4
  43.1 0.7 add_convert_fusion
  43.8 2.3 %collective-permute-start.5 = (bf16[32,128]{1,0:T(8,128)(2,1)S(1)}, bf16[32,128]{1,0:T(8,128)(2,1)S(1)}, u32[]{:S(2)}, u32[]{:S(2)}) collective-permute-start(bf16[32,128]{1,0:T(8,128)(2,1)S(1)} %add_convert_fusion), channel_id=1, source_target_pairs={{0,2},{1,3},{2,0},{3,1},{4,6},{5,7},{6,4},{7,5},{8,10},{9,11},{10,... | collective-permute-start | bytes 24584 | tf_op jit(solution)/shard_map/ppermute | solution.py:304
  46.1 6.6 %slice_bitcast_fusion = bf16[248,32,8,32]{0,3,1,2:T(8,128)(2,1)} fusion(bf16[255,8,32,32]{0,3,2,1:T(8,128)(2,1)} %param.14), kind=kLoop, calls=%fused_computation.3 | loop fusion | bytes 8126464 | tf_op jit(solution)/shard_map/transpose | solution.py:308
  52.7 7.6 %copy.33 = bf16[128,6,64,64]{0,3,1,2:T(8,128)(2,1)} copy(bf16[128,6,64,64]{0,3,2,1:T(8,128)(2,1)} %param.18) | data formatting | bytes 12582912 | tf_op jit(solution)/shard_map/optimization_barrier | solution.py:299
  60.3 9.0 %copy.34.b_hbm = bf16[128,64,384]{2,1,0:T(8,128)(2,1)} copy(bf16[128,64,384]{0,2,1:T(8,128)(2,1)} %bitcast.39) | data formatting | bytes 12582912 | tf_op jit(solution)/shard_map/reshape | solution.py:306
  69.3 4.9 %copy.35 = bf16[248,32,8,32]{0,3,2,1:T(8,128)(2,1)} copy(bf16[248,32,8,32]{0,3,1,2:T(8,128)(2,1)} %slice_bitcast_fusion) | data formatting | bytes 8126464 | tf_op jit(solution)/shard_map/transpose | solution.py:308
  74.2 7.6 %copy.36.s_hbm = bf16[248,32,256]{2,1,0:T(8,128)(2,1)} copy(bf16[248,32,256]{0,2,1:T(8,128)(2,1)} %bitcast.40) | data formatting | bytes 8126464 | tf_op jit(solution)/shard_map/reshape | solution.py:308
  81.8 7.9 %collective-permute-done.5 = bf16[32,128]{1,0:T(8,128)(2,1)S(1)} collective-permute-done((bf16[32,128]{1,0:T(8,128)(2,1)S(1)}, bf16[32,128]{1,0:T(8,128)(2,1)S(1)}, u32[]{:S(2)}, u32[]{:S(2)}) %collective-permute-start.5) | collective-permute-done | bytes 8224 | tf_op jit(solution)/shard_map/ppermute | solution.py:304
  89.7 0.1 collective-permute-start.6
  89.8 6.0 %prepare_down.1 = (bf16[7936,128]{1,0:T(8,128)(2,1)}, bf16[8192,128]{1,0:T(8,128)(2,1)}) custom-call(bf16[62,32,256]{2,1,0:T(8,128)(2,1)} %pad_maximum_fusion.g_ref, bf16[4,32,256]{2,1,0:T(8,128)(2,1)} %pad_maximum_fusion.2.low_ref), custom_call_target="tpu_custom_call" | custom-call | flops 400000000 | bytes 5000000 | tf_op jit(solution)/shard_map/prepare_down/pallas_call | solution.py:312
  95.7 0.0 collective-permute-done.6
  95.7 3.0 %collective-permute-start.7 = (bf16[128,128]{1,0:T(8,128)(2,1)S(1)}, bf16[128,128]{1,0:T(8,128)(2,1)S(1)}, u32[]{:S(2)}, u32[]{:S(2)}) collective-permute-start(bf16[128,128]{1,0:T(8,128)(2,1)S(1)} %pad_maximum_fusion.4), channel_id=1, source_target_pairs={{0,8},{1,9},{2,10},{3,11},{4,12},{5,13},{6,14},{7,15},{8,0},{9,1},... | collective-permute-start | bytes 98312 | tf_op jit(solution)/shard_map/ppermute | solution.py:304
  98.8 0.1 copy.37
  98.9 0.6 gather_fusion
  99.4 0.1 gather.12
  99.5 1.8 %collective-permute-done.7 = bf16[128,128]{1,0:T(8,128)(2,1)S(1)} collective-permute-done((bf16[128,128]{1,0:T(8,128)(2,1)S(1)}, bf16[128,128]{1,0:T(8,128)(2,1)S(1)}, u32[]{:S(2)}, u32[]{:S(2)}) %collective-permute-start.7) | collective-permute-done | bytes 32800 | tf_op jit(solution)/shard_map/ppermute | solution.py:304
  101.4 2.4 %collective-permute-start.8 = (bf16[256,128]{1,0:T(8,128)(2,1)S(1)}, bf16[256,128]{1,0:T(8,128)(2,1)S(1)}, u32[]{:S(2)}, u32[]{:S(2)}) collective-permute-start(bf16[256,128]{1,0:T(8,128)(2,1)S(1)} %pad_maximum_fusion.3), channel_id=1, source_target_pairs={{0,16},{1,17},{2,18},{3,19},{4,20},{5,21},{6,22},{7,23},{8,24},{9,... | collective-permute-start | bytes 196616 | tf_op jit(solution)/shard_map/ppermute | solution.py:304
  103.8 0.6 compare_select_fusion.pos_ref
  104.4 1.1 gather_fusion.2
  105.5 0.6 gather_fusion.1
  106.1 0.1 copy.39
  106.2 0.8 reshape.102.s_ref
  107.0 0.8 copy.40
  107.8 0.2 copy.38
  108.0 0.8 reshape.101.up_ref
  108.8 0.1 copy.24
  108.9 0.7 reshape.90.far_pos
  109.6 0.1 copy.23
  109.7 0.7 reshape.89.near_pos
  110.5 0.0 collective-permute-done.8
  110.5 0.7 pad_maximum_fusion.1.g_ref
  111.2 2.7 %top_tree.1.down_hbm = bf16[128,128]{1,0:T(8,128)(2,1)} custom-call(s32[24]{0:T(128)} %compare_select_fusion.pos_ref, bf16[512,128]{1,0:T(8,128)(2,1)} %pad_maximum_fusion.1.g_ref, bf16[3,32,256]{2,1,0:T(8,128)(2,1)} %reshape.101.up_ref, bf16[3,32,256]{2,1,0:T(8,128)(2,1)} %reshape.102.s_ref, bf16[3,32,32]{2,1,0:T(8,128)(2,1)} %gather_fusion.2, ...), custom_call_target="tpu_custom_call" | custom-call | flops 50000000 | bytes 1000000 | tf_op jit(solution)/shard_map/top_tree/pallas_call | solution.py:339
  113.9 0.0 collective-permute-done.2.gb_hbm
  113.9 0.0 collective-permute-done.xb_hbm
  113.9 0.0 collective-permute-done.1.xa_hbm
  113.9 28.7 %near_and_far.1 = bf16[8192,128]{1,0:T(8,128)(2,1)} custom-call(s32[768]{0:T(1024)} %reshape.89.near_pos, s32[1984]{0:T(1024)} %reshape.90.far_pos, bf16[8192,128]{1,0:T(8,128)(2,1)} %collective-permute-done.xb_hbm, bf16[8192,128]{1,0:T(8,128)(2,1)} %xo_hbm.1, bf16[8192,128]{1,0:T(8,128)(2,1)} %collective-permute-done.1.xa_hbm, ...), custom_call_target="tpu_custom_call" | custom-call | flops 4000000000 | bytes 30000000 | tf_op jit(solution)/shard_map/near_and_far/pallas_call | solution.py:360
  (30 shorter events, 0.2 us)
Async XLA Ops:
  0.0 105.5 %copy-start = (bf16[32,8,32,32]{3,2,1,0:T(8,128)(2,1)S(1)}, bf16[32,8,32,32]{3,2,1,0:T(8,128)(2,1)}, u32[]{:S(2)}) copy-start(bf16[32,8,32,32]{3,2,1,0:T(8,128)(2,1)} %param.16) | copy-start | bytes 1572868
  10.9 15.8 %copy-start.1 = (bf16[255,32,32]{0,2,1:T(8,128)(2,1)S(1)}, bf16[255,32,32]{0,2,1:T(8,128)(2,1)}, u32[]{:S(2)}) copy-start(bf16[255,32,32]{0,2,1:T(8,128)(2,1)} %param.12) | copy-start | bytes 1566724
  15.2 14.6 %slice-start = ((bf16[255,32,32]{0,2,1:T(8,128)(2,1)}), bf16[1,32,32]{0,2,1:T(8,128)(2,1)S(1)}, s32[]{:S(2)}) async-start(bf16[255,32,32]{0,2,1:T(8,128)(2,1)} %param.12), calls=%async_computation | async-start | bytes 524288 | tf_op jit(solution)/shard_map/slice | solution.py:279
  15.2 98.7 %collective-permute-start.2 = (bf16[62,32,256]{2,1,0:T(8,128)(2,1)}, bf16[62,32,256]{2,1,0:T(8,128)(2,1)}, u32[]{:S(2)}, u32[]{:S(2)}) collective-permute-start(bf16[62,32,256]{2,1,0:T(8,128)(2,1)} %pad_maximum_fusion.g_ref), channel_id=1, source_target_pairs={{0,1},{1,2},{2,3},{3,4},{4,5},{5,6},{6,7},{7,8},{8,9},{9,10},{10,1... | collective-permute-start | bytes 3047432 | tf_op jit(solution)/shard_map/ppermute | solution.py:271
  18.6 95.2 %collective-permute-start.3 = (bf16[62,32,256]{2,1,0:T(8,128)(2,1)}, bf16[62,32,256]{2,1,0:T(8,128)(2,1)}, u32[]{:S(2)}, u32[]{:S(2)}) collective-permute-start(bf16[62,32,256]{2,1,0:T(8,128)(2,1)} %pad_maximum_fusion.g_ref), channel_id=1, source_target_pairs={{1,0},{2,1},{3,2},{4,3},{5,4},{6,5},{7,6},{8,7},{9,8},{10,9},{11,1... | collective-permute-start | bytes 3047432 | tf_op jit(solution)/shard_map/ppermute | solution.py:272
  19.9 94.0 %collective-permute-start = (bf16[8192,128]{1,0:T(8,128)(2,1)}, bf16[8192,128]{1,0:T(8,128)(2,1)}, u32[]{:S(2)}, u32[]{:S(2)}) collective-permute-start(bf16[8192,128]{1,0:T(8,128)(2,1)} %xo_hbm.1), channel_id=1, source_target_pairs={{0,1},{1,2},{2,3},{3,4},{4,5},{5,6},{6,7},{7,8},{8,9},{9,10},{10,1... | collective-permute-start | bytes 6291464 | tf_op jit(solution)/shard_map/ppermute | solution.py:263
  25.4 88.4 %collective-permute-start.1 = (bf16[8192,128]{1,0:T(8,128)(2,1)}, bf16[8192,128]{1,0:T(8,128)(2,1)}, u32[]{:S(2)}, u32[]{:S(2)}) collective-permute-start(bf16[8192,128]{1,0:T(8,128)(2,1)} %xo_hbm.1), channel_id=1, source_target_pairs={{1,0},{2,1},{3,2},{4,3},{5,4},{6,5},{7,6},{8,7},{9,8},{10,9},{11,1... | collective-permute-start | bytes 6291464 | tf_op jit(solution)/shard_map/ppermute | solution.py:264
  29.3 12.8 %copy-start.4 = (s32[255,8]{0,1:T(8,128)S(1)}, s32[255,8]{0,1:T(8,128)}, u32[]{:S(2)}) copy-start(s32[255,8]{0,1:T(8,128)} %param.15) | copy-start | bytes 24484
  29.3 12.8 %copy-start.6 = (s32[128,6]{0,1:T(8,128)S(1)}, s32[128,6]{0,1:T(8,128)}, u32[]{:S(2)}) copy-start(s32[128,6]{0,1:T(8,128)} %param.19) | copy-start | bytes 9220
  40.9 2.2 %collective-permute-start.4 = (f32[32,128]{1,0:T(8,128)}, f32[32,128]{1,0:T(8,128)S(1)}, u32[]{:S(2)}, u32[]{:S(2)}) collective-permute-start(f32[32,128]{1,0:T(8,128)} %get-tuple-element.20), channel_id=1, source_target_pairs={{0,1},{1,0},{2,3},{3,2},{4,5},{5,4},{6,7},{7,6},{8,9},{9,8},{10,11... | collective-permute-start | bytes 49160 | tf_op jit(solution)/shard_map/ppermute | solution.py:294
  43.8 45.9 %collective-permute-start.5 = (bf16[32,128]{1,0:T(8,128)(2,1)S(1)}, bf16[32,128]{1,0:T(8,128)(2,1)S(1)}, u32[]{:S(2)}, u32[]{:S(2)}) collective-permute-start(bf16[32,128]{1,0:T(8,128)(2,1)S(1)} %add_convert_fusion), channel_id=1, source_target_pairs={{0,2},{1,3},{2,0},{3,1},{4,6},{5,7},{6,4},{7,5},{8,10},{9,11},{10,... | collective-permute-start | bytes 24584 | tf_op jit(solution)/shard_map/ppermute | solution.py:304
  74.2 24.6 %copy-start.5 = (s32[32,8]{0,1:T(8,128)S(1)}, s32[32,8]{0,1:T(8,128)}, u32[]{:S(2)}) copy-start(s32[32,8]{0,1:T(8,128)} %param.17) | copy-start | bytes 3076
  74.2 30.2 %copy-start.3 = (bf16[32,32,32]{2,1,0:T(8,128)(2,1)S(1)}, bf16[32,32,32]{2,1,0:T(8,128)(2,1)}, u32[]{:S(2)}) copy-start(bf16[32,32,32]{2,1,0:T(8,128)(2,1)} %param.13) | copy-start | bytes 196612
  81.8 25.2 %copy-start.2 = (bf16[8,32,32]{0,2,1:T(8,128)(2,1)S(1)}, bf16[8,32,32]{0,2,1:T(8,128)(2,1)}, u32[]{:S(2)}) copy-start(bf16[8,32,32]{0,2,1:T(8,128)(2,1)} %get-tuple-element.35) | copy-start | bytes 49156
  81.8 26.0 %slice-start.1 = ((bf16[32,32,32]{2,1,0:T(8,128)(2,1)}), bf16[24,32,32]{2,1,0:T(8,128)(2,1)S(1)}, s32[]{:S(2)}) async-start(bf16[32,32,32]{2,1,0:T(8,128)(2,1)} %param.13), calls=%async_computation.1 | async-start | bytes 393216 | tf_op jit(solution)/shard_map/slice | solution.py:348
  89.7 6.0 %collective-permute-start.6 = (bf16[64,128]{1,0:T(8,128)(2,1)S(1)}, bf16[64,128]{1,0:T(8,128)(2,1)S(1)}, u32[]{:S(2)}, u32[]{:S(2)}) collective-permute-start(bf16[64,128]{1,0:T(8,128)(2,1)S(1)} %pad_maximum_fusion.5), channel_id=1, source_target_pairs={{0,4},{1,5},{2,6},{3,7},{4,0},{5,1},{6,2},{7,3},{8,12},{9,13},{10,... | collective-permute-start | bytes 49160 | tf_op jit(solution)/shard_map/ppermute | solution.py:304
  95.7 5.6 %collective-permute-start.7 = (bf16[128,128]{1,0:T(8,128)(2,1)S(1)}, bf16[128,128]{1,0:T(8,128)(2,1)S(1)}, u32[]{:S(2)}, u32[]{:S(2)}) collective-permute-start(bf16[128,128]{1,0:T(8,128)(2,1)S(1)} %pad_maximum_fusion.4), channel_id=1, source_target_pairs={{0,8},{1,9},{2,10},{3,11},{4,12},{5,13},{6,14},{7,15},{8,0},{9,1},... | collective-permute-start | bytes 98312 | tf_op jit(solution)/shard_map/ppermute | solution.py:304
  101.4 9.1 %collective-permute-start.8 = (bf16[256,128]{1,0:T(8,128)(2,1)S(1)}, bf16[256,128]{1,0:T(8,128)(2,1)S(1)}, u32[]{:S(2)}, u32[]{:S(2)}) collective-permute-start(bf16[256,128]{1,0:T(8,128)(2,1)S(1)} %pad_maximum_fusion.3), channel_id=1, source_target_pairs={{0,16},{1,17},{2,18},{3,19},{4,20},{5,21},{6,22},{7,23},{8,24},{9,... | collective-permute-start | bytes 196616 | tf_op jit(solution)/shard_map/ppermute | solution.py:304

commit v4 on v3

--- a/solution.py
+++ b/solution.py
@@ -206,7 +206,7 @@
                 parts = [
                     win[rows_at(far_pos[node * slots + s] * rank, rank), :] for s in range(slots)
                 ]
-                fars.append(dot(s_ref[node], jnp.concatenate(parts, axis=0)))
+                fars.append(dot(s_ref[node + 7], jnp.concatenate(parts, axis=0)))
             total_now = total_now + jnp.concatenate(fars, axis=0)
             down[rows_at((2**k - 4) * rank + i * 256, 256), :] = total_now.astype(BF)
             return carry
@@ -291,24 +291,37 @@
         cost_estimate=pl.CostEstimate(flops=600_000_000, bytes_accessed=5_000_000, transcendentals=0),
         name="own_up",
     )(points, g_own, low_up)
+    steps = jnp.arange(2, top_depth)
+    ancestors = (devices + own) >> (top_depth - steps)
+    lists = top_lists[ancestors]
+    top_pos = jnp.where(lists >= 0, lists, 0).reshape(-1)
+    s_top = top_coupling[ancestors].transpose(0, 2, 1, 3).reshape(top_depth - 2, rank, -1)
+    e_top = top_transfer[ancestors]
+    low_down = local_transfer[:8].reshape(8 * rank, rank)
+    up_top = grouped_up(top_transfer[8:])
+    first_leaf = (own - 1) * leaf_dev
+    near_pos = jnp.where(near_lists >= 0, near_lists - first_leaf, 3 * leaf_dev).reshape(-1)
+    far_lists = local_lists[7:]
+    row = jnp.arange(7, 2 * leaf_dev - 1)
+    width = jnp.zeros_like(row)
+    for k in range(3, depth + 1):
+        width = jnp.where(row >= 2**k - 1, 2**k, width)
+    start = 3 * (width - 8) - (own - 1) * width
+    far_pos = jnp.where(far_lists >= 0, far_lists + start[:, None], 3 * nodes).reshape(-1)
     other = lax.ppermute(root_term, "leaf", [(i, i ^ 1) for i in range(devices)])
     gathered = (root_term + other).astype(BF)
     for bit in range(1, top_depth):
         flip = 2**bit
         if bit == 1:
-            near_blocks, local_coupling, gathered = lax.optimization_barrier(
-                (near_blocks, local_coupling, gathered)
+            near_blocks, local_coupling, g_late, gathered = lax.optimization_barrier(
+                (near_blocks, local_coupling, g_own, gathered)
             )
-        if bit == 2:
-            g_late, gathered = lax.optimization_barrier((g_own, gathered))
         other = lax.ppermute(gathered, "leaf", [(i, i ^ flip) for i in range(devices)])
         if bit == 1:
             near_cat = near_blocks.transpose(0, 2, 1, 3).reshape(leaf_dev, size, -1)
             near_cat = with_layout_constraint(near_cat, Layout((0, 1, 2)))
-            s_cat = local_coupling[7:].transpose(0, 2, 1, 3).reshape(nodes, rank, -1)
+            s_cat = local_coupling.transpose(0, 2, 1, 3).reshape(2 * leaf_dev - 1, rank, -1)
             s_cat = with_layout_constraint(s_cat, Layout((0, 1, 2)))
-            near_cat, s_cat, other = lax.optimization_barrier((near_cat, s_cat, other))
-        if bit == 2:
             e_groups, basis_groups = pl.pallas_call(
                 prep_kernel,
                 out_shape=(
@@ -321,21 +334,22 @@
                 cost_estimate=pl.CostEstimate(flops=400_000_000, bytes_accessed=5_000_000, transcendentals=0),
                 name="prepare_down",
             )(g_late, low_up)
-            e_groups, basis_groups, other = lax.optimization_barrier(
-                (e_groups, basis_groups, other)
+            near_cat, s_cat, e_groups, basis_groups, other = lax.optimization_barrier(
+                (near_cat, s_cat, e_groups, basis_groups, other)
+            )
+            g_before, g_after, other = lax.optimization_barrier(
+                (g_before, g_after, other)
+            )
+            top_pos, s_top, e_top, up_top, low_down, near_pos, far_pos, other = (
+                lax.optimization_barrier(
+                    (top_pos, s_top, e_top, up_top, low_down, near_pos, far_pos, other)
+                )
             )
         upper = (own & flip) > 0
         gathered = jnp.concatenate(
             [jnp.where(upper, other, gathered), jnp.where(upper, gathered, other)], axis=0
         )
 
-    steps = jnp.arange(2, top_depth)
-    ancestors = (devices + own) >> (top_depth - steps)
-    lists = top_lists[ancestors]
-    top_pos = jnp.where(lists >= 0, lists, 0).reshape(-1)
-    s_top = top_coupling[ancestors].transpose(0, 2, 1, 3).reshape(top_depth - 2, rank, -1)
-    e_top = top_transfer[ancestors]
-    low_down = local_transfer[:8].reshape(8 * rank, rank)
     down_two = pl.pallas_call(
         functools.partial(top_kernel, rank, top_depth),
         out_shape=jax.ShapeDtypeStruct((4 * rank, vecs), BF),
@@ -345,17 +359,8 @@
         compiler_params=PARAMS,
         cost_estimate=pl.CostEstimate(flops=50_000_000, bytes_accessed=1_000_000, transcendentals=0),
         name="top_tree",
-    )(top_pos, gathered, grouped_up(top_transfer[8:]), s_top, e_top, low_down)
-
-    first_leaf = (own - 1) * leaf_dev
-    near_pos = jnp.where(near_lists >= 0, near_lists - first_leaf, 3 * leaf_dev).reshape(-1)
-    far_lists = local_lists[7:]
-    row = jnp.arange(7, 2 * leaf_dev - 1)
-    width = jnp.zeros_like(row)
-    for k in range(3, depth + 1):
-        width = jnp.where(row >= 2**k - 1, 2**k, width)
-    start = 3 * (width - 8) - (own - 1) * width
-    far_pos = jnp.where(far_lists >= 0, far_lists + start[:, None], 3 * nodes).reshape(-1)
+    )(top_pos, gathered, up_top, s_top, e_top, low_down)
+
     any_space = pl.BlockSpec(memory_space=pl.ANY)
     return pl.pallas_call(
         functools.partial(field_kernel, rank, leaf_dev, size),

time: 144 us -> 136 us (0.944)
  local copies, waits for them, and re-layouts: 59.4 us -> 52.9 us
    transpose x2 -> x1, local copies, waits for them, and re-layouts: 11.5 us -> 4.89 us  [shards(): local_coupling.transpose(0, 2, 1, 3).reshape(2 * leaf_dev - 1, rank, -1)]
    transpose x5 -> x6, local copies, waits for them, and re-layouts: 2.28 us -> 3.19 us  [padded(): flat = rows.transpose(2, 0, 1).reshape(rank, -1)]
    unnamed x18 -> x20, local copies, waits for them, and re-layouts: 5.93 us -> 5.93 us
  transfers between devices with their start and end apart: 9 -> 9, of which waited for: 3 -> 4; matrix products, arithmetic and copies ran while one was open for 34% -> 31% of each run, Pallas kernels for 13% -> 13%
where the time goes in v4:
time: 136 us; the launch traced here: 135 us
  local copies, waits for them, and re-layouts  52.9 us (39%)
  Pallas kernels  46.8 us (34%)
  starting transfers between devices  19.9 us (15%)
  waiting for transfers between devices  11 us (8%)
  other arithmetic  4.06 us (3%)
    pallas_call x1, Pallas kernels, shards(): pl.pallas_call(functools.partial(field_kernel, rank, leaf_dev, size), out...  28.7 us
    ppermute x4, waiting for transfers between devices, shards(): lax.ppermute(gathered, 'leaf', [(i, i ^ flip) for i in range(devices)])  11 us
    pallas_call x1, Pallas kernels, shards(): pl.pallas_call(functools.partial(own_kernel, rank, leaf_dev), out_shape=(...  9.44 us
    reshape x1, local copies, waits for them, and re-layouts, shards(): near_cat = near_blocks.transpose(0, 2, 1, 3).reshape(leaf_dev, size, -1)  8.98 us
    reshape x1, local copies, waits for them, and re-layouts, shards(): local_coupling.transpose(0, 2, 1, 3).reshape(2 * leaf_dev - 1, rank, -1)  7.66 us
    optimization_barrier x1, local copies, waits for them, and re-layouts, shards(): lax.optimization_barrier((near_blocks, local_coupling, g_own, gathered))  7.62 us
    ppermute x4, starting transfers between devices, shards(): lax.ppermute(gathered, 'leaf', [(i, i ^ flip) for i in range(devices)])  7.1 us
    pallas_call x1, Pallas kernels, shards(): pl.pallas_call(prep_kernel, out_shape=(jax.ShapeDtypeStruct((nodes * rank...  5.93 us
  transfers between devices with their start and end apart: 9, of which 4 were waited for; matrix products, arithmetic and copies ran while one was open for 31% of the time, Pallas kernels for 13%

profile of v4, /device:TPU:0, one launch (start us, length us, event | category | flops | bytes accessed | tf_op | source)
XLA Modules:
  0.0 135.0 jit_solution(10930378827820530746)
XLA Ops:
  0.0 1.4 %slice.27 = bf16[240,32,32]{0,2,1:T(8,128)(2,1)S(1)} slice(bf16[255,32,32]{0,2,1:T(8,128)(2,1)} %param.12), slice={[15:255], [0:32], [0:32]} | slice | bytes 983040 | tf_op jit(solution)/shard_map/slice | solution.py:270
  1.5 2.6 %copy.42 = bf16[240,32,32]{2,1,0:T(8,128)(2,1)} copy(bf16[240,32,32]{0,2,1:T(8,128)(2,1)S(1)} %slice.27) | data formatting | bytes 983040
  4.1 2.5 %copy.41 = bf16[30,32,256]{2,1,0:T(8,128)(2,1)} copy(bf16[30,32,256]{1,2,0:T(8,128)(2,1)} %bitcast.40) | data formatting | bytes 983040 | tf_op jit(solution)/shard_map/reshape | solution.py:239
  6.6 2.8 %copy.29 = bf16[128,64,32]{1,2,0:T(8,128)(2,1)S(1)} copy(bf16[128,64,32]{0,2,1:T(8,128)(2,1)} %param.11) | data formatting | bytes 1048576 | tf_op args[1]
  9.4 1.5 %copy.30 = bf16[32,32,4,64]{3,2,1,0:T(4,128)(2,1)} copy(bf16[32,32,4,64]{3,1,2,0:T(8,128)(2,1)S(1)} %bitcast.42) | data formatting | bytes 1048576 | tf_op jit(solution)/shard_map/transpose | solution.py:267
  10.9 2.1 %reshape.96 = bf16[32,32,256]{2,1,0:T(8,128)(2,1)S(1)} reshape(bf16[32,32,4,64]{3,2,1,0:T(4,128)(2,1)} %copy.30) | data formatting | bytes 1048576 | tf_op jit(solution)/shard_map/reshape | solution.py:268
  13.1 2.1 %pad_maximum_fusion.g_ref = bf16[62,32,256]{2,1,0:T(8,128)(2,1)} fusion(bf16[30,32,256]{2,1,0:T(8,128)(2,1)} %copy.41, bf16[32,32,256]{2,1,0:T(8,128)(2,1)S(1)} %reshape.96), kind=kLoop, calls=%fused_computation.3 | loop fusion | flops 507904 | bytes 2031616 | tf_op jit(solution)/shard_map/concatenate | solution.py:270
  15.2 3.5 %collective-permute-start = (bf16[62,32,256]{2,1,0:T(8,128)(2,1)}, bf16[62,32,256]{2,1,0:T(8,128)(2,1)}, u32[]{:S(2)}, u32[]{:S(2)}) collective-permute-start(bf16[62,32,256]{2,1,0:T(8,128)(2,1)} %pad_maximum_fusion.g_ref), channel_id=1, source_target_pairs={{0,1},{1,2},{2,3},{3,4},{4,5},{5,6},{6,7},{7,8},{8,9},{9,10},{10,1... | collective-permute-start | bytes 3047432 | tf_op jit(solution)/shard_map/ppermute | solution.py:271
  18.7 1.3 collective-permute-start.1
  20.0 5.4 %collective-permute-start.4 = (bf16[8192,128]{1,0:T(8,128)(2,1)}, bf16[8192,128]{1,0:T(8,128)(2,1)}, u32[]{:S(2)}, u32[]{:S(2)}) collective-permute-start(bf16[8192,128]{1,0:T(8,128)(2,1)} %xo_hbm.1), channel_id=1, source_target_pairs={{0,1},{1,2},{2,3},{3,4},{4,5},{5,6},{6,7},{7,8},{8,9},{9,10},{10,1... | collective-permute-start | bytes 6291464 | tf_op jit(solution)/shard_map/ppermute | solution.py:263
  25.4 1.5 %collective-permute-start.5 = (bf16[8192,128]{1,0:T(8,128)(2,1)}, bf16[8192,128]{1,0:T(8,128)(2,1)}, u32[]{:S(2)}, u32[]{:S(2)}) collective-permute-start(bf16[8192,128]{1,0:T(8,128)(2,1)} %xo_hbm.1), channel_id=1, source_target_pairs={{1,0},{2,1},{3,2},{4,3},{5,4},{6,5},{7,6},{8,7},{9,8},{10,9},{11,1... | collective-permute-start | bytes 6291464 | tf_op jit(solution)/shard_map/ppermute | solution.py:264
  26.9 0.9 slice_bitcast_fusion.2
  27.8 0.1 slice_bitcast_fusion
  27.9 0.1 slice_bitcast_fusion.1
  28.1 1.2 copy.33
  29.3 0.1 stack.15
  29.4 0.0 copy-start.6
  29.5 0.4 copy.35
  29.8 0.0 copy-start.7
  29.8 0.0 copy-start.3
  29.9 0.1 reshape.100
  29.9 0.4 copy.43
  30.3 0.4 copy.34
  30.7 0.1 reshape.99
  30.8 0.6 pad_maximum_fusion.2.low_ref
  31.5 9.4 %own_up.1 = (bf16[7936,128]{1,0:T(8,128)(2,1)}, f32[32,128]{1,0:T(8,128)}) custom-call(bf16[8192,128]{1,0:T(8,128)(2,1)} %xo_hbm.1, bf16[62,32,256]{2,1,0:T(8,128)(2,1)} %pad_maximum_fusion.g_ref, bf16[4,32,256]{2,1,0:T(8,128)(2,1)} %pad_maximum_fusion.2.low_ref), custom_call_target="tpu_custom_call" | custom-call | flops 600000000 | bytes 5000000 | tf_op jit(solution)/shard_map/own_up/pallas_call | solution.py:282
  40.9 1.1 collective-permute-start.2
  42.1 0.1 copy.23
  42.2 0.6 gather_fusion
  42.7 0.1 gather.12
  42.8 0.1 add_select_fusion
  42.9 0.5 compare_select_fusion.pos_ref
  43.4 1.2 gather_fusion.2
  44.6 0.6 gather_fusion.1
  45.2 0.1 copy.24
  45.2 0.8 reshape.89.s_ref
  46.0 0.1 copy.28
  46.2 0.7 reshape.94.far_pos
  46.9 0.1 copy.27
  47.0 0.7 reshape.93.near_pos
  47.7 0.8 copy.26
  48.5 0.2 copy.25
  48.7 0.8 reshape.91.up_ref
  49.5 0.0 collective-permute-done.2
  49.5 2.4 %collective-permute-start.3 = (bf16[32,128]{1,0:T(8,128)(2,1)S(1)}, bf16[32,128]{1,0:T(8,128)(2,1)S(1)}, u32[]{:S(2)}, u32[]{:S(2)}) collective-permute-start(bf16[32,128]{1,0:T(8,128)(2,1)S(1)} %add_convert_fusion), channel_id=1, source_target_pairs={{0,2},{1,3},{2,0},{3,1},{4,6},{5,7},{6,4},{7,5},{8,10},{9,11},{10,... | collective-permute-start | bytes 24584 | tf_op jit(solution)/shard_map/ppermute | solution.py:319
  51.9 5.9 %prepare_down.1 = (bf16[7936,128]{1,0:T(8,128)(2,1)}, bf16[8192,128]{1,0:T(8,128)(2,1)}) custom-call(bf16[62,32,256]{2,1,0:T(8,128)(2,1)} %pad_maximum_fusion.g_ref, bf16[4,32,256]{2,1,0:T(8,128)(2,1)} %pad_maximum_fusion.2.low_ref), custom_call_target="tpu_custom_call" | custom-call | flops 400000000 | bytes 5000000 | tf_op jit(solution)/shard_map/prepare_down/pallas_call | solution.py:325
  57.8 7.6 %copy.37 = bf16[128,6,64,64]{0,3,1,2:T(8,128)(2,1)} copy(bf16[128,6,64,64]{0,3,2,1:T(8,128)(2,1)} %param.18) | data formatting | bytes 12582912 | tf_op jit(solution)/shard_map/optimization_barrier | solution.py:316
  65.4 9.0 %copy.38.b_hbm = bf16[128,64,384]{2,1,0:T(8,128)(2,1)} copy(bf16[128,64,384]{0,2,1:T(8,128)(2,1)} %bitcast.38) | data formatting | bytes 12582912 | tf_op jit(solution)/shard_map/reshape | solution.py:321
  74.4 4.9 %copy.39 = bf16[255,32,8,32]{0,3,2,1:T(8,128)(2,1)} copy(bf16[255,32,8,32]{0,3,1,2:T(8,128)(2,1)} %bitcast.41) | data formatting | bytes 8355840 | tf_op jit(solution)/shard_map/transpose | solution.py:323
  79.3 7.7 %copy.40.s_hbm = bf16[255,32,256]{2,1,0:T(8,128)(2,1)} copy(bf16[255,32,256]{0,2,1:T(8,128)(2,1)} %bitcast.39) | data formatting | bytes 8355840 | tf_op jit(solution)/shard_map/reshape | solution.py:323
  87.0 2.7 %collective-permute-done.3 = bf16[32,128]{1,0:T(8,128)(2,1)S(1)} collective-permute-done((bf16[32,128]{1,0:T(8,128)(2,1)S(1)}, bf16[32,128]{1,0:T(8,128)(2,1)S(1)}, u32[]{:S(2)}, u32[]{:S(2)}) %collective-permute-start.3) | collective-permute-done | bytes 8224 | tf_op jit(solution)/shard_map/ppermute | solution.py:319
  89.7 0.0 collective-permute-done.gb_hbm
  89.7 0.0 collective-permute-done.1.ga_hbm
  89.7 0.1 collective-permute-start.6
  89.8 3.7 %collective-permute-done.6 = bf16[64,128]{1,0:T(8,128)(2,1)S(1)} collective-permute-done((bf16[64,128]{1,0:T(8,128)(2,1)S(1)}, bf16[64,128]{1,0:T(8,128)(2,1)S(1)}, u32[]{:S(2)}, u32[]{:S(2)}) %collective-permute-start.6) | collective-permute-done | bytes 16416 | tf_op jit(solution)/shard_map/ppermute | solution.py:319
  93.5 1.6 %collective-permute-start.7 = (bf16[128,128]{1,0:T(8,128)(2,1)S(1)}, bf16[128,128]{1,0:T(8,128)(2,1)S(1)}, u32[]{:S(2)}, u32[]{:S(2)}) collective-permute-start(bf16[128,128]{1,0:T(8,128)(2,1)S(1)} %pad_maximum_fusion.4), channel_id=1, source_target_pairs={{0,8},{1,9},{2,10},{3,11},{4,12},{5,13},{6,14},{7,15},{8,0},{9,1},... | collective-permute-start | bytes 98312 | tf_op jit(solution)/shard_map/ppermute | solution.py:319
  95.2 2.3 %collective-permute-done.7 = bf16[128,128]{1,0:T(8,128)(2,1)S(1)} collective-permute-done((bf16[128,128]{1,0:T(8,128)(2,1)S(1)}, bf16[128,128]{1,0:T(8,128)(2,1)S(1)}, u32[]{:S(2)}, u32[]{:S(2)}) %collective-permute-start.7) | collective-permute-done | bytes 32800 | tf_op jit(solution)/shard_map/ppermute | solution.py:319
  97.5 3.0 %collective-permute-start.8 = (bf16[256,128]{1,0:T(8,128)(2,1)S(1)}, bf16[256,128]{1,0:T(8,128)(2,1)S(1)}, u32[]{:S(2)}, u32[]{:S(2)}) collective-permute-start(bf16[256,128]{1,0:T(8,128)(2,1)S(1)} %pad_maximum_fusion.3), channel_id=1, source_target_pairs={{0,16},{1,17},{2,18},{3,19},{4,20},{5,21},{6,22},{7,23},{8,24},{9,... | collective-permute-start | bytes 196616 | tf_op jit(solution)/shard_map/ppermute | solution.py:319
  100.5 2.2 %collective-permute-done.8 = bf16[256,128]{1,0:T(8,128)(2,1)S(1)} collective-permute-done((bf16[256,128]{1,0:T(8,128)(2,1)S(1)}, bf16[256,128]{1,0:T(8,128)(2,1)S(1)}, u32[]{:S(2)}, u32[]{:S(2)}) %collective-permute-start.8) | collective-permute-done | bytes 65568 | tf_op jit(solution)/shard_map/ppermute | solution.py:319
  102.8 0.7 pad_maximum_fusion.1.g_ref
  103.5 2.7 %top_tree.1.down_hbm = bf16[128,128]{1,0:T(8,128)(2,1)} custom-call(s32[24]{0:T(128)} %compare_select_fusion.pos_ref, bf16[512,128]{1,0:T(8,128)(2,1)} %pad_maximum_fusion.1.g_ref, bf16[3,32,256]{2,1,0:T(8,128)(2,1)} %reshape.91.up_ref, bf16[3,32,256]{2,1,0:T(8,128)(2,1)} %reshape.89.s_ref, bf16[3,32,32]{2,1,0:T(8,128)(2,1)} %gather_fusion.2, ...), custom_call_target="tpu_custom_call" | custom-call | flops 50000000 | bytes 1000000 | tf_op jit(solution)/shard_map/top_tree/pallas_call | solution.py:353
  106.2 0.0 collective-permute-done.4.xb_hbm
  106.2 0.0 collective-permute-done.5.xa_hbm
  106.2 28.7 %near_and_far.1 = bf16[8192,128]{1,0:T(8,128)(2,1)} custom-call(s32[768]{0:T(1024)} %reshape.93.near_pos, s32[1984]{0:T(1024)} %reshape.94.far_pos, bf16[8192,128]{1,0:T(8,128)(2,1)} %collective-permute-done.4.xb_hbm, bf16[8192,128]{1,0:T(8,128)(2,1)} %xo_hbm.1, bf16[8192,128]{1,0:T(8,128)(2,1)} %collective-permute-done.5.xa_hbm, ...), custom_call_target="tpu_custom_call" | custom-call | flops 4000000000 | bytes 30000000 | tf_op jit(solution)/shard_map/near_and_far/pallas_call | solution.py:365
  (31 shorter events, 0.2 us)
Async XLA Ops:
  0.0 44.6 %copy-start = (bf16[32,8,32,32]{3,2,1,0:T(8,128)(2,1)S(1)}, bf16[32,8,32,32]{3,2,1,0:T(8,128)(2,1)}, u32[]{:S(2)}) copy-start(bf16[32,8,32,32]{3,2,1,0:T(8,128)(2,1)} %param.16) | copy-start | bytes 1572868
  10.9 16.0 %copy-start.1 = (bf16[255,32,32]{0,2,1:T(8,128)(2,1)S(1)}, bf16[255,32,32]{0,2,1:T(8,128)(2,1)}, u32[]{:S(2)}) copy-start(bf16[255,32,32]{0,2,1:T(8,128)(2,1)} %param.12) | copy-start | bytes 1566724
  15.2 14.8 %slice-start = ((bf16[255,32,32]{0,2,1:T(8,128)(2,1)}), bf16[1,32,32]{0,2,1:T(8,128)(2,1)S(1)}, s32[]{:S(2)}) async-start(bf16[255,32,32]{0,2,1:T(8,128)(2,1)} %param.12), calls=%async_computation | async-start | bytes 524288 | tf_op jit(solution)/shard_map/slice | solution.py:279
  15.2 74.5 %collective-permute-start = (bf16[62,32,256]{2,1,0:T(8,128)(2,1)}, bf16[62,32,256]{2,1,0:T(8,128)(2,1)}, u32[]{:S(2)}, u32[]{:S(2)}) collective-permute-start(bf16[62,32,256]{2,1,0:T(8,128)(2,1)} %pad_maximum_fusion.g_ref), channel_id=1, source_target_pairs={{0,1},{1,2},{2,3},{3,4},{4,5},{5,6},{6,7},{7,8},{8,9},{9,10},{10,1... | collective-permute-start | bytes 3047432 | tf_op jit(solution)/shard_map/ppermute | solution.py:271
  18.7 71.0 %collective-permute-start.1 = (bf16[62,32,256]{2,1,0:T(8,128)(2,1)}, bf16[62,32,256]{2,1,0:T(8,128)(2,1)}, u32[]{:S(2)}, u32[]{:S(2)}) collective-permute-start(bf16[62,32,256]{2,1,0:T(8,128)(2,1)} %pad_maximum_fusion.g_ref), channel_id=1, source_target_pairs={{1,0},{2,1},{3,2},{4,3},{5,4},{6,5},{7,6},{8,7},{9,8},{10,9},{11,1... | collective-permute-start | bytes 3047432 | tf_op jit(solution)/shard_map/ppermute | solution.py:272
  20.0 86.2 %collective-permute-start.4 = (bf16[8192,128]{1,0:T(8,128)(2,1)}, bf16[8192,128]{1,0:T(8,128)(2,1)}, u32[]{:S(2)}, u32[]{:S(2)}) collective-permute-start(bf16[8192,128]{1,0:T(8,128)(2,1)} %xo_hbm.1), channel_id=1, source_target_pairs={{0,1},{1,2},{2,3},{3,4},{4,5},{5,6},{6,7},{7,8},{8,9},{9,10},{10,1... | collective-permute-start | bytes 6291464 | tf_op jit(solution)/shard_map/ppermute | solution.py:263
  25.4 80.8 %collective-permute-start.5 = (bf16[8192,128]{1,0:T(8,128)(2,1)}, bf16[8192,128]{1,0:T(8,128)(2,1)}, u32[]{:S(2)}, u32[]{:S(2)}) collective-permute-start(bf16[8192,128]{1,0:T(8,128)(2,1)} %xo_hbm.1), channel_id=1, source_target_pairs={{1,0},{2,1},{3,2},{4,3},{5,4},{6,5},{7,6},{8,7},{9,8},{10,9},{11,1... | collective-permute-start | bytes 6291464 | tf_op jit(solution)/shard_map/ppermute | solution.py:264
  29.4 12.6 %copy-start.6 = (s32[32,8]{0,1:T(8,128)S(1)}, s32[32,8]{0,1:T(8,128)}, u32[]{:S(2)}) copy-start(s32[32,8]{0,1:T(8,128)} %param.17) | copy-start | bytes 3076
  29.8 13.0 %copy-start.5 = (s32[255,8]{0,1:T(8,128)S(1)}, s32[255,8]{0,1:T(8,128)}, u32[]{:S(2)}) copy-start(s32[255,8]{0,1:T(8,128)} %param.15) | copy-start | bytes 24484
  29.8 13.1 %copy-start.7 = (s32[128,6]{0,1:T(8,128)S(1)}, s32[128,6]{0,1:T(8,128)}, u32[]{:S(2)}) copy-start(s32[128,6]{0,1:T(8,128)} %param.19) | copy-start | bytes 9220
  29.8 13.6 %copy-start.3 = (bf16[32,32,32]{2,1,0:T(8,128)(2,1)S(1)}, bf16[32,32,32]{2,1,0:T(8,128)(2,1)}, u32[]{:S(2)}) copy-start(bf16[32,32,32]{2,1,0:T(8,128)(2,1)} %param.13) | copy-start | bytes 196612
  31.5 16.2 %copy-start.2 = (bf16[8,32,32]{0,2,1:T(8,128)(2,1)S(1)}, bf16[8,32,32]{0,2,1:T(8,128)(2,1)}, u32[]{:S(2)}) copy-start(bf16[8,32,32]{0,2,1:T(8,128)(2,1)} %get-tuple-element.54) | copy-start | bytes 49156
  31.5 17.0 %slice-start.1 = ((bf16[32,32,32]{2,1,0:T(8,128)(2,1)}), bf16[24,32,32]{2,1,0:T(8,128)(2,1)S(1)}, s32[]{:S(2)}) async-start(bf16[32,32,32]{2,1,0:T(8,128)(2,1)} %param.13), calls=%async_computation.1 | async-start | bytes 393216 | tf_op jit(solution)/shard_map/slice | solution.py:301
  40.9 8.6 %copy-start.4 = (f32[32,128]{1,0:T(8,128)S(1)}, f32[32,128]{1,0:T(8,128)}, u32[]{:S(2)}) copy-start(f32[32,128]{1,0:T(8,128)} %get-tuple-element.29) | copy-start | bytes 49156
  40.9 8.5 %collective-permute-start.2 = (f32[32,128]{1,0:T(8,128)}, f32[32,128]{1,0:T(8,128)S(1)}, u32[]{:S(2)}, u32[]{:S(2)}) collective-permute-start(f32[32,128]{1,0:T(8,128)} %get-tuple-element.29), channel_id=1, source_target_pairs={{0,1},{1,0},{2,3},{3,2},{4,5},{5,4},{6,7},{7,6},{8,9},{9,8},{10,11... | collective-permute-start | bytes 49160 | tf_op jit(solution)/shard_map/ppermute | solution.py:311
  49.5 40.2 %collective-permute-start.3 = (bf16[32,128]{1,0:T(8,128)(2,1)S(1)}, bf16[32,128]{1,0:T(8,128)(2,1)S(1)}, u32[]{:S(2)}, u32[]{:S(2)}) collective-permute-start(bf16[32,128]{1,0:T(8,128)(2,1)S(1)} %add_convert_fusion), channel_id=1, source_target_pairs={{0,2},{1,3},{2,0},{3,1},{4,6},{5,7},{6,4},{7,5},{8,10},{9,11},{10,... | collective-permute-start | bytes 24584 | tf_op jit(solution)/shard_map/ppermute | solution.py:319
  89.7 3.8 %collective-permute-start.6 = (bf16[64,128]{1,0:T(8,128)(2,1)S(1)}, bf16[64,128]{1,0:T(8,128)(2,1)S(1)}, u32[]{:S(2)}, u32[]{:S(2)}) collective-permute-start(bf16[64,128]{1,0:T(8,128)(2,1)S(1)} %pad_maximum_fusion.5), channel_id=1, source_target_pairs={{0,4},{1,5},{2,6},{3,7},{4,0},{5,1},{6,2},{7,3},{8,12},{9,13},{10,... | collective-permute-start | bytes 49160 | tf_op jit(solution)/shard_map/ppermute | solution.py:319
  93.5 4.0 %collective-permute-start.7 = (bf16[128,128]{1,0:T(8,128)(2,1)S(1)}, bf16[128,128]{1,0:T(8,128)(2,1)S(1)}, u32[]{:S(2)}, u32[]{:S(2)}) collective-permute-start(bf16[128,128]{1,0:T(8,128)(2,1)S(1)} %pad_maximum_fusion.4), channel_id=1, source_target_pairs={{0,8},{1,9},{2,10},{3,11},{4,12},{5,13},{6,14},{7,15},{8,0},{9,1},... | collective-permute-start | bytes 98312 | tf_op jit(solution)/shard_map/ppermute | solution.py:319
  97.5 5.2 %collective-permute-start.8 = (bf16[256,128]{1,0:T(8,128)(2,1)S(1)}, bf16[256,128]{1,0:T(8,128)(2,1)S(1)}, u32[]{:S(2)}, u32[]{:S(2)}) collective-permute-start(bf16[256,128]{1,0:T(8,128)(2,1)S(1)} %pad_maximum_fusion.3), channel_id=1, source_target_pairs={{0,16},{1,17},{2,18},{3,19},{4,20},{5,21},{6,22},{7,23},{8,24},{9,... | collective-permute-start | bytes 196616 | tf_op jit(solution)/shard_map/ppermute | solution.py:319
